TPU v7x, 256 devices: a whole 4x4x8 slice. The times are simulated.
256 devices in a mesh: blk: 32 (over y_lo, z, core), head: 8 (over x, y_hi).
Axes of the slice: x: 4, y: 4 (y_hi: 2, y_lo: 2; y = y_hi * 2 + y_lo), z: 8, core: 2. Of those that a mesh axis runs over, the one named last changes fastest.
Arguments:
- queries: bfloat16 [2048, 128, 128], P('blk', 'head'), may hold values from -6 to 6
- unrotated_key_rows: bfloat16 [2048, 8, 128], P('blk', 'head'), may hold values from -6 to 6
- incoming_value_rows: bfloat16 [2048, 8, 128], P('blk', 'head'), may hold values from -6 to 6
- cache_keys: bfloat16 [32, 16, 8, 256, 128], P('blk', None, 'head'), may hold values from -135 to 135
- stored_value_rows: bfloat16 [32, 16, 8, 256, 128], P('blk', None, 'head'), may hold values from -6 to 6
- cache_len: int32 [32, 16], P('blk'), may hold values from 32 to 256, as said below
- new_count: int32 [16], replicated, may hold values from 1 to 128, 1280 in all
- slot_index: int32 [32, 16, 4], replicated, may hold values from 0 to 127, as said below
- out_weight: bfloat16 [16384, 16384], P('head', 'blk'), may hold values from -0.5 to 0.5
Outputs:
- projected: bfloat16 [2048, 16384], P('head', 'blk')
Inputs may be any that keep to these rules, and one draw needn't show every extreme that they name: `slot_index`: for every conversation each index from 0 to 127 stands in exactly one slot. `cache_len`: in every conversation some shard is full.
All inputs are finite; a program needn't handle non-finite values.
Results may differ from a plain program's by a relative error of at most 0.019.
Values may be sent and summed in bfloat16 or wider, within the bound.
No kernel may reach another device: no remote copies, remote signals or barrier semaphores. Data moves between devices by JAX's collectives and lax.ppermute only.
A program may use at most 128 MiB of HBM per device.

v0:
```python
import jax
import jax.numpy as jnp
from jax import lax
from jax.sharding import PartitionSpec as P


def shifted(block, axis, distance):
    devices = range(lax.axis_size(axis))
    route = [((i - distance) % len(devices), i) for i in devices]
    return lax.ppermute(block, axis, route)


def rotate(values, positions):
    half_width = values.shape[-1] // 2
    inverse = 1.0 / 500000.0 ** (
        jnp.arange(0, values.shape[-1], 2, dtype=jnp.float32) / values.shape[-1]
    )
    angles = positions[..., None] * inverse
    cosine = jnp.cos(angles)
    sine_part = jnp.sin(angles)
    first_half = values[..., :half_width]
    second_half = values[..., half_width:]
    return jnp.concatenate(
        [
            first_half * cosine - second_half * sine_part,
            second_half * cosine + first_half * sine_part,
        ],
        -1,
    )


def attend(
    queries_here,
    query_index,
    running,
    keys_cache,
    values_cache,
    cache_allowed,
    keys_new,
    values_new,
    new_index,
    token_count,
):
    weighted, maxima, totals = running
    scaling = queries_here.shape[-1] ** (-0.5)
    cache_scores = (
        jnp.einsum(
            "cskgd,ckld->cskgl", queries_here, keys_cache, preferred_element_type=jnp.float32
        )
        * scaling
    )
    cache_scores = jnp.where(cache_allowed[:, None, None, None, :], cache_scores, -jnp.inf)
    new_scores = (
        jnp.einsum("cskgd,ctkd->cskgt", queries_here, keys_new, preferred_element_type=jnp.float32)
        * scaling
    )
    new_allowed = (new_index[:, None, :] < token_count[:, None, None]) & (
        new_index[:, None, :] <= query_index[:, :, None]
    )
    new_scores = jnp.where(new_allowed[:, :, None, None, :], new_scores, -jnp.inf)
    block_top = jnp.maximum(jnp.max(cache_scores, -1), jnp.max(new_scores, -1))
    raised = jnp.maximum(maxima, block_top)
    shrink = jnp.exp(maxima - raised)
    cache_weights = jnp.exp(cache_scores - raised[..., None])
    new_weights = jnp.exp(new_scores - raised[..., None])
    totals = totals * shrink + jnp.sum(cache_weights, -1) + jnp.sum(new_weights, -1)
    weighted = weighted * shrink[..., None]
    weighted = weighted + jnp.einsum(
        "cskgl,ckld->cskgd",
        cache_weights.astype(jnp.bfloat16),
        values_cache,
        preferred_element_type=jnp.float32,
    )
    weighted = weighted + jnp.einsum(
        "cskgt,ctkd->cskgd",
        new_weights.astype(jnp.bfloat16),
        values_new,
        preferred_element_type=jnp.float32,
    )
    return (weighted, raised, totals)


def pass_queries(visiting):
    return shifted(visiting, "blk", 1)


def move_sums(running):
    return shifted(running, "blk", 1)


def body(
    queries,
    unrotated_key_rows,
    incoming_value_rows,
    cache_keys,
    stored_value_rows,
    cache_len,
    new_count,
    slot_index,
    out_weight,
):
    cycle_size = lax.axis_size("blk")
    device_here = lax.axis_index("blk")
    conv_count = cache_len.shape[1]
    slot_count = slot_index.shape[2]
    kv_here = unrotated_key_rows.shape[1]
    heads_here = queries.shape[1]
    query_group_width = heads_here // kv_here
    head_width = queries.shape[2]
    cache_totals = lax.psum(cache_len[0].astype(jnp.float32), "blk")
    own_index = lax.dynamic_index_in_dim(slot_index, device_here, 0, keepdims=False)
    positions = cache_totals[:, None] + own_index.astype(jnp.float32)
    queries_rot = rotate(
        queries.reshape(conv_count, slot_count, kv_here, query_group_width, head_width).astype(
            jnp.float32
        ),
        positions[:, :, None, None],
    ).astype(jnp.bfloat16)
    keys_rot = rotate(
        unrotated_key_rows.reshape(conv_count, slot_count, kv_here, head_width).astype(jnp.float32),
        positions[:, :, None],
    ).astype(jnp.bfloat16)
    values_new = incoming_value_rows.reshape(conv_count, slot_count, kv_here, head_width)
    keys_cache = cache_keys[0]
    values_cache = stored_value_rows[0]
    cache_allowed = jnp.arange(keys_cache.shape[2])[None, :] < cache_len[0][:, None]
    shape_rows = (conv_count, slot_count, kv_here, query_group_width)
    empty_state = (
        jnp.zeros(shape_rows + (head_width,), jnp.float32),
        jnp.full(shape_rows, -jnp.inf, jnp.float32),
        jnp.zeros(shape_rows, jnp.float32),
    )

    def visit_block(visiting, anchor, running):
        query_index = lax.dynamic_index_in_dim(slot_index, anchor, 0, keepdims=False)
        return attend(
            visiting,
            query_index,
            running,
            keys_cache,
            values_cache,
            cache_allowed,
            keys_rot,
            values_new,
            own_index,
            new_count,
        )

    def cycle_step(turn_index, carried):
        visiting, running = carried
        visiting = pass_queries(visiting)
        running = move_sums(running)
        anchor = (device_here - turn_index) % cycle_size
        return (visiting, visit_block(visiting, anchor, running))

    running = visit_block(queries_rot, device_here, empty_state)
    visiting, running = lax.fori_loop(1, cycle_size, cycle_step, (queries_rot, running))
    weighted, maxima, totals = move_sums(running)
    valid_rows = own_index < new_count[:, None]
    attended = jnp.where(valid_rows[:, :, None, None, None], weighted / totals[..., None], 0.0)
    attended = attended.astype(jnp.bfloat16).reshape(
        conv_count * slot_count, heads_here * head_width
    )
    partial_rows = jnp.dot(
        lax.all_gather(attended, "blk", axis=0, tiled=True),
        out_weight,
        preferred_element_type=jnp.float32,
    )
    return lax.psum_scatter(
        partial_rows.astype(jnp.bfloat16), "head", scatter_dimension=0, tiled=True
    )


def solution(mesh):
    return jax.shard_map(
        body,
        mesh=mesh,
        in_specs=(
            P("blk", "head", None),
            P("blk", "head", None),
            P("blk", "head", None),
            P("blk", None, "head", None, None),
            P("blk", None, "head", None, None),
            P("blk", None),
            P(),
            P(),
            P("head", "blk"),
        ),
        out_specs=P("head", "blk"),
        check_vma=False,
    )
```

profile of v0, /device:TPU:1, one launch (start us, length us, event | category | flops | bytes accessed | tf_op | source)
XLA Modules:
  0.0 775.6 jit_solution(13227630614752131711)
XLA Ops:
  7.4 57.1 %psum.7 = f32[16]{0:T(128)S(1)} all-reduce(f32[16]{0:T(128)S(1)} %bitcast_convert_fusion), channel_id=1, replica_groups=mesh['blk'=32,'head'=8] {'blk'}, use_global_device_ids=true, to_apply=%region_0.0 | all-reduce | flops 16 | bytes 128 | tf_op jit(solution)/shard_map/psum | solution.py:110
  77.1 514.0 %while.22 = (s32[]{:T(128)}, bf16[16,4,1,16,128]{4,3,1,0,2:T(8,128)(2,1)}, f32[16,4,1,16,128]{4,3,1,0,2:T(8,128)}, f32[16,4,1,16]{3,1,0,2:T(4,128)S(1)}, f32[16,...) while((s32[]{:T(128)}, ...), condition=%wide.region_10.11_spmd.clone, body=%wide.region_5.10_spmd.clone.sunk | while | flops 138579520 | bytes 16002660 | solution.py:157
  79.4 3.1 collective-permute-done
  90.3 2.5 collective-permute-start.3
  94.0 5.0 collective-permute-done
  108.7 7.1 collective-permute-done
  123.3 9.2 %collective-permute-done = bf16[16,4,1,16,128]{4,3,1,0,2:T(8,128)(2,1)S(1)} collective-permute-done((bf16[16,4,1,16,128]{4,3,1,0,2:T(8,128)(2,1)}, bf16[16,4,1,16,128]{4,3,1,0,2:T(8,128)(2,1)S(1)}, u32[]{:S(2)}, u32[]{:S(2)}) %collective-permute-start) | collective-permute-done | bytes 262176 | tf_op jit(solution)/shard_map/while/body/eval_jaxpr/ppermute | solution.py:10
  140.7 8.6 %collective-permute-done = bf16[16,4,1,16,128]{4,3,1,0,2:T(8,128)(2,1)S(1)} collective-permute-done((bf16[16,4,1,16,128]{4,3,1,0,2:T(8,128)(2,1)}, bf16[16,4,1,16,128]{4,3,1,0,2:T(8,128)(2,1)S(1)}, u32[]{:S(2)}, u32[]{:S(2)}) %collective-permute-start) | collective-permute-done | bytes 262176 | tf_op jit(solution)/shard_map/while/body/eval_jaxpr/ppermute | solution.py:10
  156.2 2.8 collective-permute-start.2
  160.0 6.1 collective-permute-done
  172.9 2.5 collective-permute-start
  176.7 6.1 collective-permute-done
  189.7 2.5 collective-permute-start
  193.5 6.1 collective-permute-done
  210.2 6.1 collective-permute-done
  227.0 6.1 collective-permute-done
  243.8 6.1 collective-permute-done
  260.5 6.1 collective-permute-done
  273.5 2.5 collective-permute-start
  277.3 6.1 collective-permute-done
  290.2 2.5 collective-permute-start
  294.0 6.1 collective-permute-done
  310.8 6.1 collective-permute-done
  327.6 6.1 collective-permute-done
  344.3 6.1 collective-permute-done
  361.1 6.1 collective-permute-done
  374.0 2.5 collective-permute-start
  377.8 6.1 collective-permute-done
  390.8 2.5 collective-permute-start
  394.6 6.1 collective-permute-done
  411.4 6.1 collective-permute-done
  428.1 6.1 collective-permute-done
  444.9 6.1 collective-permute-done
  461.6 6.1 collective-permute-done
  474.6 2.5 collective-permute-start
  478.4 6.1 collective-permute-done
  491.3 2.5 collective-permute-start
  495.1 6.1 collective-permute-done
  511.9 6.1 collective-permute-done
  528.7 6.1 collective-permute-done
  545.4 6.1 collective-permute-done
  562.2 6.1 collective-permute-done
  575.1 2.5 collective-permute-start
  579.0 6.1 collective-permute-done
  591.9 10.2 %collective-permute-done.5 = f32[16,4,1,16]{3,1,0,2:T(4,128)S(1)} collective-permute-done((f32[16,4,1,16]{3,1,0,2:T(4,128)}, f32[16,4,1,16]{3,1,0,2:T(4,128)S(1)}, u32[]{:S(2)}, u32[]{:S(2)}) %collective-permute-start.5) | collective-permute-done | bytes 4128 | tf_op jit(solution)/shard_map/ppermute | solution.py:10
  603.2 77.8 %all-gather.2.cloned.1.call-done = bf16[2048,2048]{1,0:T(8,128)(2,1)} async-done(((bf16[64,2048]{1,0:T(8,128)(2,1)}), bf16[2048,2048]{1,0:T(8,128)(2,1)}) %all-gather.2.cloned.1.call-update) | async-done | bytes 8388624 | tf_op jit(solution)/shard_map/all_gather | solution.py:165
  681.0 9.1 %convolution_convert_fusion = bf16[2048,512]{1,0:T(8,128)(2,1)} fusion(bf16[2048,2048]{1,0:T(8,128)(2,1)} %all-gather.2.cloned.1.call-done, bf16[2048,512]{1,0:T(8,128)(2,1)S(1)} %copy-done), kind=kOutput, calls=%fused_computation.36 | convolution fusion | flops 4296015872 | bytes 12582912 | tf_op jit(solution)/shard_map/dot_general | solution.py:164
  690.2 78.6 %reduce-scatter.2.cloned.1.call-done = bf16[256,512]{1,0:T(8,128)(2,1)} async-done(((bf16[2048,512]{1,0:T(8,128)(2,1)}), bf16[256,512]{1,0:T(8,128)(2,1)}) %reduce-scatter.2.cloned.1.call-update) | async-done | bytes 262160 | tf_op jit(solution)/shard_map/reduce_scatter | solution.py:169
  (936 shorter events, 307.1 us)
Async XLA Ops:
  6.5 674.5 %all-gather.2.cloned.1.call-start = ((), (), s32[]{:S(2)}) async-start(), calls=%async_computation.1 | async-start | bytes 8650752 | tf_op jit(solution)/shard_map/all_gather | solution.py:165
  90.3 11.9 %collective-permute-start.3 = (f32[16,4,1,16]{3,1,0,2:T(4,128)}, f32[16,4,1,16]{3,1,0,2:T(4,128)S(1)}, u32[]{:S(2)}, u32[]{:S(2)}) collective-permute-start(f32[16,4,1,16]{3,1,0,2:T(4,128)} %get-tuple-element.549), channel_id=1, source_target_pairs={{248,0},{0,8},{8,16},{16,24},{24,32},{32,40},{40,48},{48,56},{56,6... | collective-permute-start | bytes 12296 | tf_op jit(solution)/shard_map/while/body/eval_jaxpr/ppermute | solution.py:10
  105.0 13.9 %collective-permute-start.3 = (f32[16,4,1,16]{3,1,0,2:T(4,128)}, f32[16,4,1,16]{3,1,0,2:T(4,128)S(1)}, u32[]{:S(2)}, u32[]{:S(2)}) collective-permute-start(f32[16,4,1,16]{3,1,0,2:T(4,128)} %get-tuple-element.549), channel_id=1, source_target_pairs={{248,0},{0,8},{8,16},{16,24},{24,32},{32,40},{40,48},{48,56},{56,6... | collective-permute-start | bytes 12296 | tf_op jit(solution)/shard_map/while/body/eval_jaxpr/ppermute | solution.py:10
  107.6 12.0 %collective-permute-start.2 = (f32[16,4,1,16,128]{4,3,1,0,2:T(8,128)}, f32[16,4,1,16,128]{4,3,1,0,2:T(8,128)}, u32[]{:S(2)}, u32[]{:S(2)}) collective-permute-start(f32[16,4,1,16,128]{4,3,1,0,2:T(8,128)} %get-tuple-element.547), channel_id=1, source_target_pairs={{248,0},{0,8},{8,16},{16,24},{24,32},{32,40},{40,48},{48,56},{56,6... | collective-permute-start | bytes 1572872 | tf_op jit(solution)/shard_map/while/body/eval_jaxpr/ppermute | solution.py:10
  121.8 13.9 %collective-permute-start.3 = (f32[16,4,1,16]{3,1,0,2:T(4,128)}, f32[16,4,1,16]{3,1,0,2:T(4,128)S(1)}, u32[]{:S(2)}, u32[]{:S(2)}) collective-permute-start(f32[16,4,1,16]{3,1,0,2:T(4,128)} %get-tuple-element.549), channel_id=1, source_target_pairs={{248,0},{0,8},{8,16},{16,24},{24,32},{32,40},{40,48},{48,56},{56,6... | collective-permute-start | bytes 12296 | tf_op jit(solution)/shard_map/while/body/eval_jaxpr/ppermute | solution.py:10
  122.1 11.8 %collective-permute-start.1 = (f32[16,4,1,16]{3,1,0,2:T(4,128)S(1)}, f32[16,4,1,16]{3,1,0,2:T(4,128)S(1)}, u32[]{:S(2)}, u32[]{:S(2)}) collective-permute-start(f32[16,4,1,16]{3,1,0,2:T(4,128)S(1)} %get-tuple-element.548), channel_id=1, source_target_pairs={{248,0},{0,8},{8,16},{16,24},{24,32},{32,40},{40,48},{48,56},{56,6... | collective-permute-start | bytes 12296 | tf_op jit(solution)/shard_map/while/body/eval_jaxpr/ppermute | solution.py:10
  122.3 14.1 %collective-permute-start.2 = (f32[16,4,1,16,128]{4,3,1,0,2:T(8,128)}, f32[16,4,1,16,128]{4,3,1,0,2:T(8,128)}, u32[]{:S(2)}, u32[]{:S(2)}) collective-permute-start(f32[16,4,1,16,128]{4,3,1,0,2:T(8,128)} %get-tuple-element.547), channel_id=1, source_target_pairs={{248,0},{0,8},{8,16},{16,24},{24,32},{32,40},{40,48},{48,56},{56,6... | collective-permute-start | bytes 1572872 | tf_op jit(solution)/shard_map/while/body/eval_jaxpr/ppermute | solution.py:10
  138.5 13.9 %collective-permute-start.3 = (f32[16,4,1,16]{3,1,0,2:T(4,128)}, f32[16,4,1,16]{3,1,0,2:T(4,128)S(1)}, u32[]{:S(2)}, u32[]{:S(2)}) collective-permute-start(f32[16,4,1,16]{3,1,0,2:T(4,128)} %get-tuple-element.549), channel_id=1, source_target_pairs={{248,0},{0,8},{8,16},{16,24},{24,32},{32,40},{40,48},{48,56},{56,6... | collective-permute-start | bytes 12296 | tf_op jit(solution)/shard_map/while/body/eval_jaxpr/ppermute | solution.py:10
  138.5 12.1 %collective-permute-start.1 = (f32[16,4,1,16]{3,1,0,2:T(4,128)S(1)}, f32[16,4,1,16]{3,1,0,2:T(4,128)S(1)}, u32[]{:S(2)}, u32[]{:S(2)}) collective-permute-start(f32[16,4,1,16]{3,1,0,2:T(4,128)S(1)} %get-tuple-element.548), channel_id=1, source_target_pairs={{248,0},{0,8},{8,16},{16,24},{24,32},{32,40},{40,48},{48,56},{56,6... | collective-permute-start | bytes 12296 | tf_op jit(solution)/shard_map/while/body/eval_jaxpr/ppermute | solution.py:10
  138.7 14.4 %collective-permute-start.2 = (f32[16,4,1,16,128]{4,3,1,0,2:T(8,128)}, f32[16,4,1,16,128]{4,3,1,0,2:T(8,128)}, u32[]{:S(2)}, u32[]{:S(2)}) collective-permute-start(f32[16,4,1,16,128]{4,3,1,0,2:T(8,128)} %get-tuple-element.547), channel_id=1, source_target_pairs={{248,0},{0,8},{8,16},{16,24},{24,32},{32,40},{40,48},{48,56},{56,6... | collective-permute-start | bytes 1572872 | tf_op jit(solution)/shard_map/while/body/eval_jaxpr/ppermute | solution.py:10
  155.3 13.9 %collective-permute-start.3 = (f32[16,4,1,16]{3,1,0,2:T(4,128)}, f32[16,4,1,16]{3,1,0,2:T(4,128)S(1)}, u32[]{:S(2)}, u32[]{:S(2)}) collective-permute-start(f32[16,4,1,16]{3,1,0,2:T(4,128)} %get-tuple-element.549), channel_id=1, source_target_pairs={{248,0},{0,8},{8,16},{16,24},{24,32},{32,40},{40,48},{48,56},{56,6... | collective-permute-start | bytes 12296 | tf_op jit(solution)/shard_map/while/body/eval_jaxpr/ppermute | solution.py:10
  155.3 12.1 %collective-permute-start.1 = (f32[16,4,1,16]{3,1,0,2:T(4,128)S(1)}, f32[16,4,1,16]{3,1,0,2:T(4,128)S(1)}, u32[]{:S(2)}, u32[]{:S(2)}) collective-permute-start(f32[16,4,1,16]{3,1,0,2:T(4,128)S(1)} %get-tuple-element.548), channel_id=1, source_target_pairs={{248,0},{0,8},{8,16},{16,24},{24,32},{32,40},{40,48},{48,56},{56,6... | collective-permute-start | bytes 12296 | tf_op jit(solution)/shard_map/while/body/eval_jaxpr/ppermute | solution.py:10
  156.2 13.7 %collective-permute-start.2 = (f32[16,4,1,16,128]{4,3,1,0,2:T(8,128)}, f32[16,4,1,16,128]{4,3,1,0,2:T(8,128)}, u32[]{:S(2)}, u32[]{:S(2)}) collective-permute-start(f32[16,4,1,16,128]{4,3,1,0,2:T(8,128)} %get-tuple-element.547), channel_id=1, source_target_pairs={{248,0},{0,8},{8,16},{16,24},{24,32},{32,40},{40,48},{48,56},{56,6... | collective-permute-start | bytes 1572872 | tf_op jit(solution)/shard_map/while/body/eval_jaxpr/ppermute | solution.py:10
  172.1 13.9 %collective-permute-start.3 = (f32[16,4,1,16]{3,1,0,2:T(4,128)}, f32[16,4,1,16]{3,1,0,2:T(4,128)S(1)}, u32[]{:S(2)}, u32[]{:S(2)}) collective-permute-start(f32[16,4,1,16]{3,1,0,2:T(4,128)} %get-tuple-element.549), channel_id=1, source_target_pairs={{248,0},{0,8},{8,16},{16,24},{24,32},{32,40},{40,48},{48,56},{56,6... | collective-permute-start | bytes 12296 | tf_op jit(solution)/shard_map/while/body/eval_jaxpr/ppermute | solution.py:10
  172.1 12.1 %collective-permute-start.1 = (f32[16,4,1,16]{3,1,0,2:T(4,128)S(1)}, f32[16,4,1,16]{3,1,0,2:T(4,128)S(1)}, u32[]{:S(2)}, u32[]{:S(2)}) collective-permute-start(f32[16,4,1,16]{3,1,0,2:T(4,128)S(1)} %get-tuple-element.548), channel_id=1, source_target_pairs={{248,0},{0,8},{8,16},{16,24},{24,32},{32,40},{40,48},{48,56},{56,6... | collective-permute-start | bytes 12296 | tf_op jit(solution)/shard_map/while/body/eval_jaxpr/ppermute | solution.py:10
  188.8 13.9 %collective-permute-start.3 = (f32[16,4,1,16]{3,1,0,2:T(4,128)}, f32[16,4,1,16]{3,1,0,2:T(4,128)S(1)}, u32[]{:S(2)}, u32[]{:S(2)}) collective-permute-start(f32[16,4,1,16]{3,1,0,2:T(4,128)} %get-tuple-element.549), channel_id=1, source_target_pairs={{248,0},{0,8},{8,16},{16,24},{24,32},{32,40},{40,48},{48,56},{56,6... | collective-permute-start | bytes 12296 | tf_op jit(solution)/shard_map/while/body/eval_jaxpr/ppermute | solution.py:10
  205.6 13.9 %collective-permute-start.3 = (f32[16,4,1,16]{3,1,0,2:T(4,128)}, f32[16,4,1,16]{3,1,0,2:T(4,128)S(1)}, u32[]{:S(2)}, u32[]{:S(2)}) collective-permute-start(f32[16,4,1,16]{3,1,0,2:T(4,128)} %get-tuple-element.549), channel_id=1, source_target_pairs={{248,0},{0,8},{8,16},{16,24},{24,32},{32,40},{40,48},{48,56},{56,6... | collective-permute-start | bytes 12296 | tf_op jit(solution)/shard_map/while/body/eval_jaxpr/ppermute | solution.py:10
  222.3 13.9 %collective-permute-start.3 = (f32[16,4,1,16]{3,1,0,2:T(4,128)}, f32[16,4,1,16]{3,1,0,2:T(4,128)S(1)}, u32[]{:S(2)}, u32[]{:S(2)}) collective-permute-start(f32[16,4,1,16]{3,1,0,2:T(4,128)} %get-tuple-element.549), channel_id=1, source_target_pairs={{248,0},{0,8},{8,16},{16,24},{24,32},{32,40},{40,48},{48,56},{56,6... | collective-permute-start | bytes 12296 | tf_op jit(solution)/shard_map/while/body/eval_jaxpr/ppermute | solution.py:10
  239.1 13.9 %collective-permute-start.3 = (f32[16,4,1,16]{3,1,0,2:T(4,128)}, f32[16,4,1,16]{3,1,0,2:T(4,128)S(1)}, u32[]{:S(2)}, u32[]{:S(2)}) collective-permute-start(f32[16,4,1,16]{3,1,0,2:T(4,128)} %get-tuple-element.549), channel_id=1, source_target_pairs={{248,0},{0,8},{8,16},{16,24},{24,32},{32,40},{40,48},{48,56},{56,6... | collective-permute-start | bytes 12296 | tf_op jit(solution)/shard_map/while/body/eval_jaxpr/ppermute | solution.py:10
  255.9 13.9 %collective-permute-start.3 = (f32[16,4,1,16]{3,1,0,2:T(4,128)}, f32[16,4,1,16]{3,1,0,2:T(4,128)S(1)}, u32[]{:S(2)}, u32[]{:S(2)}) collective-permute-start(f32[16,4,1,16]{3,1,0,2:T(4,128)} %get-tuple-element.549), channel_id=1, source_target_pairs={{248,0},{0,8},{8,16},{16,24},{24,32},{32,40},{40,48},{48,56},{56,6... | collective-permute-start | bytes 12296 | tf_op jit(solution)/shard_map/while/body/eval_jaxpr/ppermute | solution.py:10
  256.4 11.6 %collective-permute-start.1 = (f32[16,4,1,16]{3,1,0,2:T(4,128)S(1)}, f32[16,4,1,16]{3,1,0,2:T(4,128)S(1)}, u32[]{:S(2)}, u32[]{:S(2)}) collective-permute-start(f32[16,4,1,16]{3,1,0,2:T(4,128)S(1)} %get-tuple-element.548), channel_id=1, source_target_pairs={{248,0},{0,8},{8,16},{16,24},{24,32},{32,40},{40,48},{48,56},{56,6... | collective-permute-start | bytes 12296 | tf_op jit(solution)/shard_map/while/body/eval_jaxpr/ppermute | solution.py:10
  272.6 13.9 %collective-permute-start.3 = (f32[16,4,1,16]{3,1,0,2:T(4,128)}, f32[16,4,1,16]{3,1,0,2:T(4,128)S(1)}, u32[]{:S(2)}, u32[]{:S(2)}) collective-permute-start(f32[16,4,1,16]{3,1,0,2:T(4,128)} %get-tuple-element.549), channel_id=1, source_target_pairs={{248,0},{0,8},{8,16},{16,24},{24,32},{32,40},{40,48},{48,56},{56,6... | collective-permute-start | bytes 12296 | tf_op jit(solution)/shard_map/while/body/eval_jaxpr/ppermute | solution.py:10
  273.1 11.6 %collective-permute-start.1 = (f32[16,4,1,16]{3,1,0,2:T(4,128)S(1)}, f32[16,4,1,16]{3,1,0,2:T(4,128)S(1)}, u32[]{:S(2)}, u32[]{:S(2)}) collective-permute-start(f32[16,4,1,16]{3,1,0,2:T(4,128)S(1)} %get-tuple-element.548), channel_id=1, source_target_pairs={{248,0},{0,8},{8,16},{16,24},{24,32},{32,40},{40,48},{48,56},{56,6... | collective-permute-start | bytes 12296 | tf_op jit(solution)/shard_map/while/body/eval_jaxpr/ppermute | solution.py:10
  289.4 13.9 %collective-permute-start.3 = (f32[16,4,1,16]{3,1,0,2:T(4,128)}, f32[16,4,1,16]{3,1,0,2:T(4,128)S(1)}, u32[]{:S(2)}, u32[]{:S(2)}) collective-permute-start(f32[16,4,1,16]{3,1,0,2:T(4,128)} %get-tuple-element.549), channel_id=1, source_target_pairs={{248,0},{0,8},{8,16},{16,24},{24,32},{32,40},{40,48},{48,56},{56,6... | collective-permute-start | bytes 12296 | tf_op jit(solution)/shard_map/while/body/eval_jaxpr/ppermute | solution.py:10
  306.1 13.9 %collective-permute-start.3 = (f32[16,4,1,16]{3,1,0,2:T(4,128)}, f32[16,4,1,16]{3,1,0,2:T(4,128)S(1)}, u32[]{:S(2)}, u32[]{:S(2)}) collective-permute-start(f32[16,4,1,16]{3,1,0,2:T(4,128)} %get-tuple-element.549), channel_id=1, source_target_pairs={{248,0},{0,8},{8,16},{16,24},{24,32},{32,40},{40,48},{48,56},{56,6... | collective-permute-start | bytes 12296 | tf_op jit(solution)/shard_map/while/body/eval_jaxpr/ppermute | solution.py:10
  322.9 13.9 %collective-permute-start.3 = (f32[16,4,1,16]{3,1,0,2:T(4,128)}, f32[16,4,1,16]{3,1,0,2:T(4,128)S(1)}, u32[]{:S(2)}, u32[]{:S(2)}) collective-permute-start(f32[16,4,1,16]{3,1,0,2:T(4,128)} %get-tuple-element.549), channel_id=1, source_target_pairs={{248,0},{0,8},{8,16},{16,24},{24,32},{32,40},{40,48},{48,56},{56,6... | collective-permute-start | bytes 12296 | tf_op jit(solution)/shard_map/while/body/eval_jaxpr/ppermute | solution.py:10
  339.7 13.9 %collective-permute-start.3 = (f32[16,4,1,16]{3,1,0,2:T(4,128)}, f32[16,4,1,16]{3,1,0,2:T(4,128)S(1)}, u32[]{:S(2)}, u32[]{:S(2)}) collective-permute-start(f32[16,4,1,16]{3,1,0,2:T(4,128)} %get-tuple-element.549), channel_id=1, source_target_pairs={{248,0},{0,8},{8,16},{16,24},{24,32},{32,40},{40,48},{48,56},{56,6... | collective-permute-start | bytes 12296 | tf_op jit(solution)/shard_map/while/body/eval_jaxpr/ppermute | solution.py:10
  356.4 13.9 %collective-permute-start.3 = (f32[16,4,1,16]{3,1,0,2:T(4,128)}, f32[16,4,1,16]{3,1,0,2:T(4,128)S(1)}, u32[]{:S(2)}, u32[]{:S(2)}) collective-permute-start(f32[16,4,1,16]{3,1,0,2:T(4,128)} %get-tuple-element.549), channel_id=1, source_target_pairs={{248,0},{0,8},{8,16},{16,24},{24,32},{32,40},{40,48},{48,56},{56,6... | collective-permute-start | bytes 12296 | tf_op jit(solution)/shard_map/while/body/eval_jaxpr/ppermute | solution.py:10
  356.9 11.6 %collective-permute-start.1 = (f32[16,4,1,16]{3,1,0,2:T(4,128)S(1)}, f32[16,4,1,16]{3,1,0,2:T(4,128)S(1)}, u32[]{:S(2)}, u32[]{:S(2)}) collective-permute-start(f32[16,4,1,16]{3,1,0,2:T(4,128)S(1)} %get-tuple-element.548), channel_id=1, source_target_pairs={{248,0},{0,8},{8,16},{16,24},{24,32},{32,40},{40,48},{48,56},{56,6... | collective-permute-start | bytes 12296 | tf_op jit(solution)/shard_map/while/body/eval_jaxpr/ppermute | solution.py:10
  373.2 13.9 %collective-permute-start.3 = (f32[16,4,1,16]{3,1,0,2:T(4,128)}, f32[16,4,1,16]{3,1,0,2:T(4,128)S(1)}, u32[]{:S(2)}, u32[]{:S(2)}) collective-permute-start(f32[16,4,1,16]{3,1,0,2:T(4,128)} %get-tuple-element.549), channel_id=1, source_target_pairs={{248,0},{0,8},{8,16},{16,24},{24,32},{32,40},{40,48},{48,56},{56,6... | collective-permute-start | bytes 12296 | tf_op jit(solution)/shard_map/while/body/eval_jaxpr/ppermute | solution.py:10
  373.7 11.6 %collective-permute-start.1 = (f32[16,4,1,16]{3,1,0,2:T(4,128)S(1)}, f32[16,4,1,16]{3,1,0,2:T(4,128)S(1)}, u32[]{:S(2)}, u32[]{:S(2)}) collective-permute-start(f32[16,4,1,16]{3,1,0,2:T(4,128)S(1)} %get-tuple-element.548), channel_id=1, source_target_pairs={{248,0},{0,8},{8,16},{16,24},{24,32},{32,40},{40,48},{48,56},{56,6... | collective-permute-start | bytes 12296 | tf_op jit(solution)/shard_map/while/body/eval_jaxpr/ppermute | solution.py:10
  389.9 13.9 %collective-permute-start.3 = (f32[16,4,1,16]{3,1,0,2:T(4,128)}, f32[16,4,1,16]{3,1,0,2:T(4,128)S(1)}, u32[]{:S(2)}, u32[]{:S(2)}) collective-permute-start(f32[16,4,1,16]{3,1,0,2:T(4,128)} %get-tuple-element.549), channel_id=1, source_target_pairs={{248,0},{0,8},{8,16},{16,24},{24,32},{32,40},{40,48},{48,56},{56,6... | collective-permute-start | bytes 12296 | tf_op jit(solution)/shard_map/while/body/eval_jaxpr/ppermute | solution.py:10
  406.7 13.9 %collective-permute-start.3 = (f32[16,4,1,16]{3,1,0,2:T(4,128)}, f32[16,4,1,16]{3,1,0,2:T(4,128)S(1)}, u32[]{:S(2)}, u32[]{:S(2)}) collective-permute-start(f32[16,4,1,16]{3,1,0,2:T(4,128)} %get-tuple-element.549), channel_id=1, source_target_pairs={{248,0},{0,8},{8,16},{16,24},{24,32},{32,40},{40,48},{48,56},{56,6... | collective-permute-start | bytes 12296 | tf_op jit(solution)/shard_map/while/body/eval_jaxpr/ppermute | solution.py:10
  423.5 13.9 %collective-permute-start.3 = (f32[16,4,1,16]{3,1,0,2:T(4,128)}, f32[16,4,1,16]{3,1,0,2:T(4,128)S(1)}, u32[]{:S(2)}, u32[]{:S(2)}) collective-permute-start(f32[16,4,1,16]{3,1,0,2:T(4,128)} %get-tuple-element.549), channel_id=1, source_target_pairs={{248,0},{0,8},{8,16},{16,24},{24,32},{32,40},{40,48},{48,56},{56,6... | collective-permute-start | bytes 12296 | tf_op jit(solution)/shard_map/while/body/eval_jaxpr/ppermute | solution.py:10
  440.2 13.9 %collective-permute-start.3 = (f32[16,4,1,16]{3,1,0,2:T(4,128)}, f32[16,4,1,16]{3,1,0,2:T(4,128)S(1)}, u32[]{:S(2)}, u32[]{:S(2)}) collective-permute-start(f32[16,4,1,16]{3,1,0,2:T(4,128)} %get-tuple-element.549), channel_id=1, source_target_pairs={{248,0},{0,8},{8,16},{16,24},{24,32},{32,40},{40,48},{48,56},{56,6... | collective-permute-start | bytes 12296 | tf_op jit(solution)/shard_map/while/body/eval_jaxpr/ppermute | solution.py:10
  457.0 13.9 %collective-permute-start.3 = (f32[16,4,1,16]{3,1,0,2:T(4,128)}, f32[16,4,1,16]{3,1,0,2:T(4,128)S(1)}, u32[]{:S(2)}, u32[]{:S(2)}) collective-permute-start(f32[16,4,1,16]{3,1,0,2:T(4,128)} %get-tuple-element.549), channel_id=1, source_target_pairs={{248,0},{0,8},{8,16},{16,24},{24,32},{32,40},{40,48},{48,56},{56,6... | collective-permute-start | bytes 12296 | tf_op jit(solution)/shard_map/while/body/eval_jaxpr/ppermute | solution.py:10
  457.5 11.6 %collective-permute-start.1 = (f32[16,4,1,16]{3,1,0,2:T(4,128)S(1)}, f32[16,4,1,16]{3,1,0,2:T(4,128)S(1)}, u32[]{:S(2)}, u32[]{:S(2)}) collective-permute-start(f32[16,4,1,16]{3,1,0,2:T(4,128)S(1)} %get-tuple-element.548), channel_id=1, source_target_pairs={{248,0},{0,8},{8,16},{16,24},{24,32},{32,40},{40,48},{48,56},{56,6... | collective-permute-start | bytes 12296 | tf_op jit(solution)/shard_map/while/body/eval_jaxpr/ppermute | solution.py:10
  473.7 13.9 %collective-permute-start.3 = (f32[16,4,1,16]{3,1,0,2:T(4,128)}, f32[16,4,1,16]{3,1,0,2:T(4,128)S(1)}, u32[]{:S(2)}, u32[]{:S(2)}) collective-permute-start(f32[16,4,1,16]{3,1,0,2:T(4,128)} %get-tuple-element.549), channel_id=1, source_target_pairs={{248,0},{0,8},{8,16},{16,24},{24,32},{32,40},{40,48},{48,56},{56,6... | collective-permute-start | bytes 12296 | tf_op jit(solution)/shard_map/while/body/eval_jaxpr/ppermute | solution.py:10
  474.3 11.6 %collective-permute-start.1 = (f32[16,4,1,16]{3,1,0,2:T(4,128)S(1)}, f32[16,4,1,16]{3,1,0,2:T(4,128)S(1)}, u32[]{:S(2)}, u32[]{:S(2)}) collective-permute-start(f32[16,4,1,16]{3,1,0,2:T(4,128)S(1)} %get-tuple-element.548), channel_id=1, source_target_pairs={{248,0},{0,8},{8,16},{16,24},{24,32},{32,40},{40,48},{48,56},{56,6... | collective-permute-start | bytes 12296 | tf_op jit(solution)/shard_map/while/body/eval_jaxpr/ppermute | solution.py:10
  490.5 13.9 %collective-permute-start.3 = (f32[16,4,1,16]{3,1,0,2:T(4,128)}, f32[16,4,1,16]{3,1,0,2:T(4,128)S(1)}, u32[]{:S(2)}, u32[]{:S(2)}) collective-permute-start(f32[16,4,1,16]{3,1,0,2:T(4,128)} %get-tuple-element.549), channel_id=1, source_target_pairs={{248,0},{0,8},{8,16},{16,24},{24,32},{32,40},{40,48},{48,56},{56,6... | collective-permute-start | bytes 12296 | tf_op jit(solution)/shard_map/while/body/eval_jaxpr/ppermute | solution.py:10
  507.2 13.9 %collective-permute-start.3 = (f32[16,4,1,16]{3,1,0,2:T(4,128)}, f32[16,4,1,16]{3,1,0,2:T(4,128)S(1)}, u32[]{:S(2)}, u32[]{:S(2)}) collective-permute-start(f32[16,4,1,16]{3,1,0,2:T(4,128)} %get-tuple-element.549), channel_id=1, source_target_pairs={{248,0},{0,8},{8,16},{16,24},{24,32},{32,40},{40,48},{48,56},{56,6... | collective-permute-start | bytes 12296 | tf_op jit(solution)/shard_map/while/body/eval_jaxpr/ppermute | solution.py:10
  524.0 13.9 %collective-permute-start.3 = (f32[16,4,1,16]{3,1,0,2:T(4,128)}, f32[16,4,1,16]{3,1,0,2:T(4,128)S(1)}, u32[]{:S(2)}, u32[]{:S(2)}) collective-permute-start(f32[16,4,1,16]{3,1,0,2:T(4,128)} %get-tuple-element.549), channel_id=1, source_target_pairs={{248,0},{0,8},{8,16},{16,24},{24,32},{32,40},{40,48},{48,56},{56,6... | collective-permute-start | bytes 12296 | tf_op jit(solution)/shard_map/while/body/eval_jaxpr/ppermute | solution.py:10
  540.8 13.9 %collective-permute-start.3 = (f32[16,4,1,16]{3,1,0,2:T(4,128)}, f32[16,4,1,16]{3,1,0,2:T(4,128)S(1)}, u32[]{:S(2)}, u32[]{:S(2)}) collective-permute-start(f32[16,4,1,16]{3,1,0,2:T(4,128)} %get-tuple-element.549), channel_id=1, source_target_pairs={{248,0},{0,8},{8,16},{16,24},{24,32},{32,40},{40,48},{48,56},{56,6... | collective-permute-start | bytes 12296 | tf_op jit(solution)/shard_map/while/body/eval_jaxpr/ppermute | solution.py:10
  557.5 13.9 %collective-permute-start.3 = (f32[16,4,1,16]{3,1,0,2:T(4,128)}, f32[16,4,1,16]{3,1,0,2:T(4,128)S(1)}, u32[]{:S(2)}, u32[]{:S(2)}) collective-permute-start(f32[16,4,1,16]{3,1,0,2:T(4,128)} %get-tuple-element.549), channel_id=1, source_target_pairs={{248,0},{0,8},{8,16},{16,24},{24,32},{32,40},{40,48},{48,56},{56,6... | collective-permute-start | bytes 12296 | tf_op jit(solution)/shard_map/while/body/eval_jaxpr/ppermute | solution.py:10
  558.0 11.6 %collective-permute-start.1 = (f32[16,4,1,16]{3,1,0,2:T(4,128)S(1)}, f32[16,4,1,16]{3,1,0,2:T(4,128)S(1)}, u32[]{:S(2)}, u32[]{:S(2)}) collective-permute-start(f32[16,4,1,16]{3,1,0,2:T(4,128)S(1)} %get-tuple-element.548), channel_id=1, source_target_pairs={{248,0},{0,8},{8,16},{16,24},{24,32},{32,40},{40,48},{48,56},{56,6... | collective-permute-start | bytes 12296 | tf_op jit(solution)/shard_map/while/body/eval_jaxpr/ppermute | solution.py:10
  574.3 13.9 %collective-permute-start.3 = (f32[16,4,1,16]{3,1,0,2:T(4,128)}, f32[16,4,1,16]{3,1,0,2:T(4,128)S(1)}, u32[]{:S(2)}, u32[]{:S(2)}) collective-permute-start(f32[16,4,1,16]{3,1,0,2:T(4,128)} %get-tuple-element.549), channel_id=1, source_target_pairs={{248,0},{0,8},{8,16},{16,24},{24,32},{32,40},{40,48},{48,56},{56,6... | collective-permute-start | bytes 12296 | tf_op jit(solution)/shard_map/while/body/eval_jaxpr/ppermute | solution.py:10
  574.8 11.6 %collective-permute-start.1 = (f32[16,4,1,16]{3,1,0,2:T(4,128)S(1)}, f32[16,4,1,16]{3,1,0,2:T(4,128)S(1)}, u32[]{:S(2)}, u32[]{:S(2)}) collective-permute-start(f32[16,4,1,16]{3,1,0,2:T(4,128)S(1)} %get-tuple-element.548), channel_id=1, source_target_pairs={{248,0},{0,8},{8,16},{16,24},{24,32},{32,40},{40,48},{48,56},{56,6... | collective-permute-start | bytes 12296 | tf_op jit(solution)/shard_map/while/body/eval_jaxpr/ppermute | solution.py:10
  603.2 165.6 %reduce-scatter.2.cloned.1.call-start = ((), (), s32[]{:S(2)}) async-start(), calls=%async_computation.2 | async-start | bytes 2359296 | tf_op jit(solution)/shard_map/reduce_scatter | solution.py:169
  (210 other events, 2301.0 us)
Sparse Core Ops, SparseCore 0:
  603.3 77.6 all-gather.1
  690.3 78.4 reduce-scatter.1
where the time goes:
time: 779 us; the launch traced here: 776 us
  waiting for transfers between devices  361 us (46%)
  matrix products  134 us (17%)
  starting transfers between devices  105 us (13%)
  blocking collectives  57.1 us (7%)
  other arithmetic  53.5 us (7%)
  local copies, waits for them, and re-layouts  49.5 us (6%)
  between operations  13.5 us (2%)
    ppermute x126, waiting for transfers between devices, shifted(): return lax.ppermute(block, axis, route)  204 us
    ppermute x126, starting transfers between devices, shifted(): return lax.ppermute(block, axis, route)  105 us
    reduce_scatter x1, waiting for transfers between devices, body(): lax.psum_scatter(partial_rows.astype(jnp.bfloat16), 'head', scatter_dimen...  78.6 us
    all_gather x1, waiting for transfers between devices, body(): lax.all_gather(attended, 'blk', axis=0, tiled=True)  77.8 us
    dot_general x32, matrix products, attend(): jnp.einsum('cskgt,ctkd->cskgd', new_weights.astype(jnp.bfloat16), values_...  68.8 us
    psum x1, blocking collectives, body(): cache_totals = lax.psum(cache_len[0].astype(jnp.float32), 'blk')  57.1 us
    dot_general x32, matrix products, attend(): jnp.einsum('cskgd,ctkd->cskgt', queries_here, keys_new, preferred_element...  24.4 us
    le x62, local copies, waits for them, and re-layouts, attend(): new_index[:, None, :] <= query_index[:, :, None]  23.5 us
  transfers between devices with their start and end apart: 128, of which 35 were waited for; matrix products, arithmetic and copies ran while one was open for 19% of the time, Pallas kernels for 0%

commit v1 on v0

v1 whole, which is shorter than its diff:
```python
import functools

import jax
import jax.numpy as jnp
from jax import lax
from jax.experimental import pallas as pl
from jax.experimental.pallas import tpu as pltpu
from jax.sharding import Mesh, PartitionSpec as P

LOG2_E = 1.4426950408889634
ROWS = 256
CLOSED = 1.0e9
LEGS = (
    ((1, 0), (0, 1), (0, -1)),
    ((1, 1), (1, -1), (0, 2), (0, -2)),
    ((1, 2), (1, -2), (0, 3), (0, -3)),
    ((1, 3), (1, -3), (0, 4), (1, 4)),
)


def attend_kernel(shards, first, last, lens_ref, q_ref, *refs):
    refs = list(refs)
    shard_refs = [refs.pop(0) for _ in range(shards)]
    if first:
        new_k_ref, new_v_ref, key_index_ref, row_index_ref = [refs.pop(0) for _ in range(4)]
    else:
        sums_in, stats_in = [refs.pop(0) for _ in range(2)]
    sums_out, stats_out = [refs.pop(0) for _ in range(2)]
    q = q_ref[0]
    scale = LOG2_E / q.shape[-1] ** 0.5
    slots = shard_refs[0].shape[0] // 2
    slot = lax.broadcasted_iota(jnp.int32, (slots, 1), 0)
    scores, values = [], []
    for i, ref in enumerate(shard_refs):
        s = lax.dot_general(
            ref[0:slots, :], q, (((1,), (1,)), ((), ())), preferred_element_type=jnp.float32
        )
        scores.append(jnp.where(slot < lens_ref[i], s * scale, -jnp.inf))
        values.append(ref[slots : 2 * slots, :])
    if first:
        s = lax.dot_general(
            new_k_ref[...], q, (((1,), (1,)), ((), ())), preferred_element_type=jnp.float32
        )
        seen = key_index_ref[:, 0:1] <= row_index_ref[0, 0:1, :]
        scores.append(jnp.where(seen, s * scale, -jnp.inf))
        values.append(new_v_ref[...])
    top = functools.reduce(jnp.maximum, [jnp.max(s, axis=0, keepdims=True) for s in scores])
    if first:
        total = jnp.zeros_like(top)
        sums = jnp.zeros((q.shape[-1], q.shape[0]), jnp.float32)
    else:
        before = stats_in[0, 0:1, :]
        top = jnp.maximum(top, before)
        shrink = jnp.exp2(before - top)
        total = stats_in[0, 1:2, :] * shrink
        sums = sums_in[0] * shrink
    for s, v in zip(scores, values):
        w = jnp.exp2(s - top)
        total = total + jnp.sum(w, axis=0, keepdims=True)
        sums = sums + lax.dot_general(
            v, w.astype(jnp.bfloat16), (((0,), (0,)), ((), ())), preferred_element_type=jnp.float32
        )
    sums_out[0] = sums
    stats_out[0] = jnp.concatenate([top, total, jnp.zeros((6, q.shape[0]), jnp.float32)], 0)
    if last:
        message = refs.pop(0)
        width = q.shape[-1]
        message[0, 0:width, :] = sums.astype(jnp.bfloat16)
        rows = []
        for value in (top, total):
            for _ in range(3):
                part = value.astype(jnp.bfloat16).astype(jnp.float32)
                rows.append(part)
                value = value - part
        rows.append(jnp.zeros((10, q.shape[0]), jnp.float32))
        message[0, width : width + 16, :] = jnp.concatenate(rows, 0).astype(jnp.bfloat16)


def attend(lens, q, shards, state, new, last):
    halves, rows, width = q.shape
    whole = lambda a: pl.BlockSpec(a.shape, lambda i, j: (0,) * a.ndim)
    lanes = lambda depth: pl.BlockSpec((1, depth, ROWS), lambda i, j: (i, 0, j))
    in_specs = [
        pl.BlockSpec(memory_space=pltpu.SMEM),
        pl.BlockSpec((1, ROWS, width), lambda i, j: (i, j, 0)),
    ]
    in_specs += [whole(a) for a in shards]
    if state is None:
        in_specs += [whole(a) for a in new[:3]] + [lanes(8)]
        extra = tuple(new)
    else:
        in_specs += [lanes(width), lanes(8)]
        extra = tuple(state)
    out_shape = [
        jax.ShapeDtypeStruct((halves, width, rows), jnp.float32),
        jax.ShapeDtypeStruct((halves, 8, rows), jnp.float32),
    ]
    out_specs = [lanes(width), lanes(8)]
    if last:
        out_shape.append(jax.ShapeDtypeStruct((halves, width + 16, rows), jnp.bfloat16))
        out_specs.append(lanes(width + 16))
    keys = sum(a.shape[0] // 2 for a in shards)
    return pl.pallas_call(
        functools.partial(attend_kernel, len(shards), state is None, last),
        grid=(halves, rows // ROWS),
        in_specs=in_specs,
        out_specs=out_specs,
        out_shape=out_shape,
        compiler_params=pltpu.CompilerParams(vmem_limit_bytes=48 * 1024 * 1024),
        cost_estimate=pl.CostEstimate(
            flops=8 * halves * rows * width * keys,
            bytes_accessed=4 * 1024 * 1024,
            transcendentals=halves * rows * keys,
        ),
    )(lens, q, *shards, *extra)


def merge_kernel(sums_ref, stats_ref, message_ref, live_ref, out_ref):
    width, rows = sums_ref.shape
    tokens = out_ref.shape[0]
    tail = message_ref[width : width + 16, :].astype(jnp.float32)
    top_a, total_a = stats_ref[0:1, :], stats_ref[1:2, :]
    top_b = tail[0:1] + tail[1:2] + tail[2:3]
    total_b = tail[3:4] + tail[4:5] + tail[5:6]
    top = jnp.maximum(top_a, top_b)
    a, b = jnp.exp2(top_a - top), jnp.exp2(top_b - top)
    inverse = live_ref[0:1, :] / (total_a * a + total_b * b)
    a, b = a * inverse, b * inverse
    for i in range(rows // 128):
        at = slice(i * 128, (i + 1) * 128)
        block = sums_ref[:, at] * a[:, at] + message_ref[0:width, at].astype(jnp.float32) * b[:, at]
        block = block.T.astype(jnp.bfloat16)
        for part in range(128 // tokens):
            head = i * (128 // tokens) + part
            out_ref[:, head * width : (head + 1) * width] = block[
                part * tokens : (part + 1) * tokens, :
            ]


def merge(sums, stats, message, live, tokens):
    width, rows = sums.shape
    return pl.pallas_call(
        merge_kernel,
        out_shape=jax.ShapeDtypeStruct((tokens, rows // tokens * width), jnp.bfloat16),
        compiler_params=pltpu.CompilerParams(vmem_limit_bytes=48 * 1024 * 1024),
        cost_estimate=pl.CostEstimate(
            flops=4 * width * rows, bytes_accessed=8 * width * rows, transcendentals=2 * rows
        ),
    )(sums, stats, message, live)


def rotate(values, cosine, sine):
    half = values.shape[-1] // 2
    first, second = values[..., :half], values[..., half:]
    return jnp.concatenate(
        [first * cosine - second * sine, second * cosine + first * sine], -1
    ).astype(jnp.bfloat16)


def body(
    queries,
    unrotated_key_rows,
    incoming_value_rows,
    cache_keys,
    stored_value_rows,
    cache_len,
    new_count,
    slot_index,
    out_weight,
):
    ny, nz, nheads = lax.axis_size("y"), lax.axis_size("z"), lax.axis_size("head")
    y, z, core = lax.axis_index("y"), lax.axis_index("z"), lax.axis_index("core")
    convs, slots = slot_index.shape[1], slot_index.shape[2]
    shards = slot_index.shape[0]
    heads, width = queries.shape[1], queries.shape[2]
    here = y * nz + z
    other_core = [(0, 1), (1, 0)]

    small = jnp.concatenate(
        [
            queries.reshape(convs, slots * heads, width),
            unrotated_key_rows.reshape(convs, slots, width),
            incoming_value_rows.reshape(convs, slots, width),
            jnp.broadcast_to(
                cache_len[0].astype(jnp.bfloat16)[:, None, None], (convs, 16 - 2 * slots, width)
            ),
        ],
        1,
    )
    mine = lax.all_to_all(small, ("y", "z"), 0, 0, tiled=True)
    theirs = lax.ppermute(mine, "core", other_core)

    def shard_of(conversation):
        return jnp.concatenate(
            [
                lax.dynamic_index_in_dim(cache_keys[0, :, 0], conversation, 0, keepdims=False),
                lax.dynamic_index_in_dim(
                    stored_value_rows[0, :, 0], conversation, 0, keepdims=False
                ),
            ],
            0,
        )

    def chip_at(dy, dz):
        return (y + dy) % ny * nz + (z + dz) % nz

    def leg(dy, dz):
        route = [
            (a * nz + b, (a + dy) % ny * nz + (b + dz) % nz) for a in range(ny) for b in range(nz)
        ]
        return lax.ppermute(shard_of(chip_at(dy, dz)), ("y", "z"), route)

    arrived = [[leg(dy, dz) for dy, dz in group] for group in LEGS]

    weight_core = lax.ppermute(out_weight, "core", other_core)
    weight_y = lax.ppermute(out_weight, "y", [(0, 1), (1, 0)])
    weight_both = lax.ppermute(weight_y, "core", other_core)
    near = [
        jnp.where(core == 0, out_weight, weight_core),
        jnp.where(core == 0, weight_core, out_weight),
    ]
    far = [
        jnp.where(core == 0, weight_y, weight_both),
        jnp.where(core == 0, weight_both, weight_y),
    ]
    weights = jnp.stack(
        [jnp.where(y == 0, a, b) for a, b in zip(near, far)]
        + [jnp.where(y == 0, b, a) for a, b in zip(near, far)]
    )

    both = jnp.where(core == 0, jnp.stack([mine, theirs], 1), jnp.stack([theirs, mine], 1))
    both = both.reshape(shards, small.shape[1], width)
    lens = both[:, slots * heads + 2 * slots, 0].astype(jnp.float32)
    base = jnp.sum(lens)
    index = lax.dynamic_index_in_dim(slot_index, here, 1, keepdims=False)
    index = index.reshape(shards, 2, slots // 2).transpose(1, 0, 2)
    live = index < new_count[here]
    inverse = 1.0 / 500000.0 ** (jnp.arange(0, width, 2, dtype=jnp.float32) / width)
    angles = (base + index.astype(jnp.float32))[..., None] * inverse
    cosine, sine = jnp.cos(angles), jnp.sin(angles)
    q = both[:, : slots * heads].reshape(shards, 2, slots // 2, heads, width)
    q = q.transpose(1, 3, 0, 2, 4).astype(jnp.float32)
    q = rotate(q, cosine[:, None], sine[:, None])
    tokens = shards * slots // 2
    q = q.reshape(2, heads * tokens, width)

    def new_rows(start):
        rows = both[:, start : start + slots].reshape(shards, 2, slots // 2, width)
        return rows.transpose(1, 0, 2, 3)

    new_k = rotate(new_rows(slots * heads).astype(jnp.float32), cosine, sine)
    new_k = new_k.reshape(2 * tokens, width)
    new_v = new_rows(slots * heads + slots).reshape(2 * tokens, width)
    kept = live & (jnp.arange(shards)[None, :, None] % 2 == core)
    key_index = jnp.where(kept, index.astype(jnp.float32), CLOSED).reshape(2 * tokens, 1)
    key_index = jnp.broadcast_to(key_index, (2 * tokens, 128))
    row_index = jnp.broadcast_to(
        index.astype(jnp.float32).reshape(2, 1, 1, tokens), (2, 8, heads, tokens)
    ).reshape(2, 8, heads * tokens)

    own_lens = mine[:, slots * heads + 2 * slots, 0].astype(jnp.int32)

    def lens_of(group):
        return jnp.stack([own_lens[chip_at(-dy, -dz)] for dy, dz in group])

    state = attend(
        lens_of([(0, 0)]), q, [shard_of(here)], None, (new_k, new_v, key_index, row_index), False
    )
    for group, blocks in zip(LEGS, arrived):
        last = group is LEGS[-1]
        state = attend(lens_of(group), q, blocks, state, None, last)
    sums, stats, message = state

    message = lax.ppermute(
        lax.dynamic_index_in_dim(message, 1 - core, 0, keepdims=False), "core", other_core
    )
    own_half = lambda a: lax.dynamic_index_in_dim(a, core, 0, keepdims=False)
    live_row = jnp.broadcast_to(
        own_half(live).astype(jnp.float32).reshape(1, 1, tokens), (8, heads, tokens)
    ).reshape(8, heads * tokens)
    attended = merge(own_half(sums), own_half(stats), message, live_row, tokens)

    attended = attended.reshape(nheads, tokens // nheads, heads * width)
    up = [(i, (i + 1) % nz) for i in range(nz)]
    down = [(i, (i - 1) % nz) for i in range(nz)]
    held = {0: attended}
    for step in range(1, nz // 2):
        held[-step % nz] = lax.ppermute(held[(1 - step) % nz], "z", up)
        held[step] = lax.ppermute(held[step - 1], "z", down)
    middle = nz // 2
    cut = nheads // 2
    if cut == 0:
        held[middle] = lax.ppermute(held[middle - 1], "z", down)
    else:
        held[middle] = jnp.concatenate(
            [
                lax.ppermute(held[middle + 1][:cut], "z", up),
                lax.ppermute(held[middle - 1][cut:], "z", down),
            ],
            0,
        )

    def project(which):
        rows = jnp.stack([held[k] for k in which], 1)
        rows = rows.reshape(-1, heads * width)
        parts = jnp.einsum("rk,wkn->wrn", rows, weights, preferred_element_type=jnp.float32)
        parts = parts.astype(jnp.bfloat16).reshape(4 * nheads, -1, out_weight.shape[1])
        got = lax.all_to_all(parts, ("y", "core", "head"), 0, 0, tiled=True)
        got = got.reshape(ny, 2, nheads, len(which), tokens // nheads, -1)
        return jnp.sum(got.astype(jnp.float32), 2).astype(jnp.bfloat16)

    early = (0, 1, 2, nz - 2, nz - 1)
    late = tuple(range(3, nz - 2))
    first, second = project(early), project(late)
    order = early + late
    done = jnp.concatenate([first, second], 2)
    done = jnp.stack([done[:, :, order.index(k)] for k in range(nz)], 0)
    done = lax.dynamic_slice_in_dim(jnp.concatenate([done, done], 0), (nz - z) % nz, nz, 0)
    done = done.reshape(nz, ny, 2, shards // nheads, slots // 2, -1)
    done = done.transpose(3, 1, 0, 2, 4, 5)
    return done.reshape(shards // nheads * convs * slots, -1)


def solution(mesh):
    blk, head = mesh.shape["blk"], mesh.shape["head"]
    fine = Mesh(mesh.devices.reshape(2, blk // 4, 2, head), ("y", "z", "core", "head"))
    blk = ("y", "z", "core")
    return jax.shard_map(
        body,
        mesh=fine,
        in_specs=(
            P(blk, "head", None),
            P(blk, "head", None),
            P(blk, "head", None),
            P(blk, None, "head", None, None),
            P(blk, None, "head", None, None),
            P(blk, None),
            P(),
            P(),
            P("head", blk),
        ),
        out_specs=P("head", blk),
        check_vma=False,
    )
```

time: 779 us -> 224 us (0.29)
  waiting for transfers between devices: 361 us -> 49.8 us
  matrix products: 134 us -> 10.1 us
  blocking collectives: 57.1 us -> 0 us
  local copies, waits for them, and re-layouts: 49.5 us -> 9.52 us
  Pallas kernels: 0 us -> 32.5 us
  starting transfers between devices: 105 us -> 81.1 us
  other arithmetic: 53.5 us -> 38.5 us
  between operations: 13.5 us -> 0.95 us
    ppermute x126 -> x28, waiting for transfers between devices: 204 us -> 21 us  [the longest x3 9.76 us: body(): held[step] = lax.ppermute(held[step - 1], 'z', down)]
    dot_general x129 -> x2, matrix products: 134 us -> 10.1 us  [project(): jnp.einsum('rk,wkn->wrn', rows, weights, preferred_element_type=jnp.float32)]
    reduce_scatter x1 -> x0, waiting for transfers between devices: 78.6 us -> none  [body(): lax.psum_scatter(partial_rows.astype(jnp.bfloat16), 'head', scatter_dimen...]
    all_gather x1 -> x0, waiting for transfers between devices: 77.8 us -> none  [body(): lax.all_gather(attended, 'blk', axis=0, tiled=True)]
    psum x1 -> x0, blocking collectives: 57.1 us -> none  [body(): cache_totals = lax.psum(cache_len[0].astype(jnp.float32), 'blk')]
    ppermute x126 -> x28, starting transfers between devices: 105 us -> 56 us  [the longest x15 29.9 us: leg(): return lax.ppermute(shard_of(chip_at(dy, dz)), ('y', 'z'), route)]
    pallas_call x0 -> x6, Pallas kernels: none -> 32.5 us  [the longest x5 32.3 us: attend(): pl.pallas_call(functools.partial(attend_kernel, len(shards), state is Non...]
    all_to_all x0 -> x3, waiting for transfers between devices: none -> 28.8 us  [the longest x2 28.8 us: project(): got = lax.all_to_all(parts, ('y', 'core', 'head'), 0, 0, tiled=True)]
  transfers between devices with their start and end apart: 128 -> 31, of which waited for: 35 -> 8; matrix products, arithmetic and copies ran while one was open for 19% -> 21% of each run, Pallas kernels for 0% -> 15%
where the time goes in v1:
time: 224 us; the launch traced here: 223 us
  starting transfers between devices  81.1 us (36%)
  waiting for transfers between devices  49.8 us (22%)
  other arithmetic  38.5 us (17%)
  Pallas kernels  32.5 us (15%)
  matrix products  10.1 us (5%)
  local copies, waits for them, and re-layouts  9.52 us (4%)
    pallas_call x5, Pallas kernels, attend(): pl.pallas_call(functools.partial(attend_kernel, len(shards), state is Non...  32.3 us
    ppermute x15, starting transfers between devices, leg(): return lax.ppermute(shard_of(chip_at(dy, dz)), ('y', 'z'), route)  29.9 us
    all_to_all x2, waiting for transfers between devices, project(): got = lax.all_to_all(parts, ('y', 'core', 'head'), 0, 0, tiled=True)  28.8 us
    concatenate x16, other arithmetic, shard_of(): jnp.concatenate([lax.dynamic_index_in_dim(cache_keys[0, :, 0], conversati...  17.6 us
    all_to_all x2, starting transfers between devices, project(): got = lax.all_to_all(parts, ('y', 'core', 'head'), 0, 0, tiled=True)  15 us
    all_to_all x1, starting transfers between devices, body(): mine = lax.all_to_all(small, ('y', 'z'), 0, 0, tiled=True)  10.1 us
    dot_general x2, matrix products, project(): jnp.einsum('rk,wkn->wrn', rows, weights, preferred_element_type=jnp.float32)  10.1 us
    ppermute x3, waiting for transfers between devices, body(): held[step] = lax.ppermute(held[step - 1], 'z', down)  9.76 us
  transfers between devices with their start and end apart: 31, of which 8 were waited for; matrix products, arithmetic and copies ran while one was open for 21% of the time, Pallas kernels for 15%

profile of v1, /device:TPU:1, one launch (start us, length us, event | category | flops | bytes accessed | tf_op | source)
XLA Modules:
  0.0 222.5 jit_solution(15251590927631254277)
XLA Ops:
  0.8 1.8 pad_maximum_fusion.7
  2.6 10.1 %all-to-all-start = ((bf16[16,80,128]{2,1,0:T(8,128)(2,1)}), bf16[16,80,128]{2,1,0:T(8,128)(2,1)S(1)}, u32[]{:S(2)}, u32[]{:S(2)}) async-start(bf16[16,80,128]{2,1,0:T(8,128)(2,1)} %pad_maximum_fusion.7), calls=%async_computation | async-start | bytes 655360 | tf_op jit(solution)/shard_map/all_to_all | solution.py:190
  13.0 2.8 %dynamic-slice_bitcast_fusion.2 = (bf16[256,128]{1,0:T(8,128)(2,1)}, bf16[256,128]{1,0:T(8,128)(2,1)S(1)}, bf16[256,128]{1,0:T(8,128)(2,1)S(1)}, bf16[256,128]{1...) fusion(bf16[1,16,1,256,128]{4,3,2,1,0:T(8,128)(2,1)S(1)} %copy-, ...), kind=kLoop, calls=%fused_computation.48 | loop fusion | bytes 4194368 | tf_op jit(solution)/shard_map/jit(dynamic_index_in_dim)/squeeze | solution.py:197
  16.4 2.1 collective-permute-start.12
  26.0 1.5 pad_maximum_fusion.8
  27.6 1.5 pad_maximum_fusion.9
  29.1 1.5 pad_maximum_fusion.10
  30.6 1.5 pad_maximum_fusion.11
  32.1 1.5 pad_maximum_fusion.12
  33.6 1.5 pad_maximum_fusion.13
  35.2 1.5 pad_maximum_fusion.14
  37.0 1.5 pad_maximum_fusion.15
  38.6 1.5 pad_maximum_fusion.17
  42.1 2.0 pad_add_fusion.3.lens_ref
  44.1 2.4 %collective-permute-start.3 = (bf16[16,80,128]{2,1,0:T(8,128)(2,1)S(1)}, bf16[16,80,128]{2,1,0:T(8,128)(2,1)S(1)}, u32[]{:S(2)}, u32[]{:S(2)}) collective-permute-start(bf16[16,80,128]{2,1,0:T(8,128)(2,1)S(1)} %all-to-all-done), channel_id=1, source_target_pairs={{0,8},{8,0},{1,9},{9,1},{2,10},{10,2},{3,11},{11,3},{4,12},{12,4},... | collective-permute-start | bytes 983048 | tf_op jit(solution)/shard_map/ppermute | solution.py:191
  46.5 2.6 %pad_add_fusion.lens_ref = s32[4]{0:T(128)S(1)} fusion(s32[1]{0:T(128)} %bitcast.11, s32[1]{0:T(128)} %bitcast.10, s32[1]{0:T(128)} %bitcast.9, s32[1]{0:T(128)} %bitcast.8), kind=kLoop, calls=%fused_computation.135 | loop fusion | flops 12 | bytes 32 | tf_op jit(solution)/shard_map/stack | solution.py:264
  49.1 2.5 %pad_add_fusion.1.lens_ref = s32[4]{0:T(128)S(1)} fusion(s32[1]{0:T(128)} %bitcast.33, s32[1]{0:T(128)} %bitcast.32, s32[1]{0:T(128)} %bitcast.31, s32[1]{0:T(128)} %bitcast.30), kind=kLoop, calls=%fused_computation.136 | loop fusion | flops 12 | bytes 32 | tf_op jit(solution)/shard_map/stack | solution.py:264
  51.6 2.6 %pad_add_fusion.2.lens_ref = s32[4]{0:T(128)S(1)} fusion(s32[1]{0:T(128)} %bitcast.45, s32[1]{0:T(128)} %bitcast.44, s32[1]{0:T(128)} %bitcast.43, s32[1]{0:T(128)} %bitcast.42), kind=kLoop, calls=%fused_computation.137 | loop fusion | flops 12 | bytes 32 | tf_op jit(solution)/shard_map/stack | solution.py:264
  61.7 4.8 %shard_map.91 = (f32[2,128,1024]{2,1,0:T(8,128)S(1)}, f32[2,8,1024]{2,1,0:T(8,128)S(1)}) custom-call(s32[1]{0:T(128)} %bitcast.63.lens_ref, bf16[2,1024,128]{2,1,0:T(8,128)(2,1)S(1)} %pad_maximum_fusion.6.q_ref, bf16[512,128]{1,0:T(8,128)(2,1)S(1)} %pad_maximum_fusion.23.refs_0_, bf16[128,128]{1,0:T(8,128)(2,1)S(1)} %pad_maximum_fusion.24.refs_1_, ...), custom_call_target="tpu_custom_call" | custom-call | flops 536870912 | bytes 4194304 | tf_op jit(solution)/shard_map/pallas_call | solution.py:103
  66.6 1.6 collective-permute-start.14
  68.2 2.0 collective-permute-start.15
  70.3 5.8 %shard_map.92 = (f32[2,128,1024]{2,1,0:T(8,128)S(1)}, f32[2,8,1024]{2,1,0:T(8,128)S(1)}) custom-call(s32[3]{0:T(128)S(1)} %pad_add_fusion.3.lens_ref, bf16[2,1024,128]{2,1,0:T(8,128)(2,1)S(1)} %pad_maximum_fusion.6.q_ref, bf16[512,128]{1,0:T(8,128)(2,1)S(1)} %collective-permute-done.16.refs_0_, bf16[512,128]{1,0:T(8,128)(2,1)S(1)} %collective-permute-done.17.refs_1_, ...), custom_call_target="tpu_custom_call" | custom-call | flops 1610612736 | bytes 4194304 | tf_op jit(solution)/shard_map/pallas_call | solution.py:103
  76.1 3.2 %collective-permute-start.8 = (bf16[512,128]{1,0:T(8,128)(2,1)S(1)}, bf16[512,128]{1,0:T(8,128)(2,1)S(1)}, u32[]{:S(2)}, u32[]{:S(2)}) collective-permute-start(bf16[512,128]{1,0:T(8,128)(2,1)S(1)} %copy-done.17), channel_id=1, source_target_pairs={{0,160},{16,176},{32,192},{48,208},{64,224},{80,240},{96,128},{112... | collective-permute-start | bytes 393224 | tf_op jit(solution)/shard_map/ppermute | solution.py:211
  79.3 1.6 collective-permute-start.9
  80.9 2.1 collective-permute-start.10
  83.0 2.4 %collective-permute-start.11 = (bf16[512,128]{1,0:T(8,128)(2,1)S(1)}, bf16[512,128]{1,0:T(8,128)(2,1)S(1)}, u32[]{:S(2)}, u32[]{:S(2)}) collective-permute-start(bf16[512,128]{1,0:T(8,128)(2,1)S(1)} %copy-done.18), channel_id=1, source_target_pairs={{0,80},{16,96},{32,112},{48,0},{64,16},{80,32},{96,48},{112,64},{1... | collective-permute-start | bytes 393224 | tf_op jit(solution)/shard_map/ppermute | solution.py:211
  85.4 7.2 %shard_map.93 = (f32[2,128,1024]{2,1,0:T(8,128)S(1)}, f32[2,8,1024]{2,1,0:T(8,128)S(1)}) custom-call(s32[4]{0:T(128)S(1)} %pad_add_fusion.2.lens_ref, bf16[2,1024,128]{2,1,0:T(8,128)(2,1)S(1)} %pad_maximum_fusion.6.q_ref, bf16[512,128]{1,0:T(8,128)(2,1)S(1)} %collective-permute-done.12.refs_0_, bf16[512,128]{1,0:T(8,128)(2,1)S(1)} %collective-permute-done.13.refs_1_, ...), custom_call_target="tpu_custom_call" | custom-call | flops 2147483648 | bytes 4194304 | tf_op jit(solution)/shard_map/pallas_call | solution.py:103
  93.5 4.5 %collective-permute-start.5 = (bf16[512,128]{1,0:T(8,128)(2,1)S(1)}, bf16[512,128]{1,0:T(8,128)(2,1)S(1)}, u32[]{:S(2)}, u32[]{:S(2)}) collective-permute-start(bf16[512,128]{1,0:T(8,128)(2,1)S(1)} %copy-done.13), channel_id=1, source_target_pairs={{0,208},{16,224},{32,240},{48,128},{64,144},{80,160},{96,176},{112... | collective-permute-start | bytes 393224 | tf_op jit(solution)/shard_map/ppermute | solution.py:211
  98.1 5.3 %collective-permute-start.6 = (bf16[512,128]{1,0:T(8,128)(2,1)S(1)}, bf16[512,128]{1,0:T(8,128)(2,1)S(1)}, u32[]{:S(2)}, u32[]{:S(2)}) collective-permute-start(bf16[512,128]{1,0:T(8,128)(2,1)S(1)} %copy-done.12), channel_id=1, source_target_pairs={{0,64},{16,80},{32,96},{48,112},{64,0},{80,16},{96,32},{112,48},{1... | collective-permute-start | bytes 393224 | tf_op jit(solution)/shard_map/ppermute | solution.py:211
  104.5 7.2 %shard_map.94 = (f32[2,128,1024]{2,1,0:T(8,128)S(1)}, f32[2,8,1024]{2,1,0:T(8,128)S(1)}) custom-call(s32[4]{0:T(128)S(1)} %pad_add_fusion.1.lens_ref, bf16[2,1024,128]{2,1,0:T(8,128)(2,1)S(1)} %pad_maximum_fusion.6.q_ref, bf16[512,128]{1,0:T(8,128)(2,1)S(1)} %collective-permute-done.8.refs_0_, bf16[512,128]{1,0:T(8,128)(2,1)S(1)} %collective-permute-done.9.refs_1_, ...), custom_call_target="tpu_custom_call" | custom-call | flops 2147483648 | bytes 4194304 | tf_op jit(solution)/shard_map/pallas_call | solution.py:103
  111.7 3.5 %collective-permute-start = (bf16[2048,512]{1,0:T(8,128)(2,1)S(1)}, bf16[2048,512]{1,0:T(8,128)(2,1)}, u32[]{:S(2)}, u32[]{:S(2)}) collective-permute-start(bf16[2048,512]{1,0:T(8,128)(2,1)S(1)} %copy-done), channel_id=1, source_target_pairs={{0,8},{8,0},{1,9},{9,1},{2,10},{10,2},{3,11},{11,3},{4,12},{12,4},... | collective-permute-start | bytes 6291464 | tf_op jit(solution)/shard_map/ppermute | solution.py:215
  115.1 7.4 %shard_map.95 = (f32[2,128,1024]{2,1,0:T(8,128)S(1)}, f32[2,8,1024]{2,1,0:T(8,128)S(1)}, bf16[2,144,1024]{2,1,0:T(8,128)(2,1)S(1)}) custom-call(s32[4]{0:T(128)S(1)} %pad_add_fusion.lens_ref, bf16[2,1024,128]{2,1,0:T(8,128)(2,1)S(1)} %pad_maximum_fusion.6.q_ref, bf16[512,128]{1,0:T(8,128)(2,1)S(1)} %collective-permute-done.4.refs_0_, ...), custom_call_target="tpu_custom_call" | custom-call | flops 2147483648 | bytes 4194304 | tf_op jit(solution)/shard_map/pallas_call | solution.py:103
  123.3 3.9 %collective-permute-start.19 = (bf16[144,1024]{1,0:T(8,128)(2,1)}, bf16[144,1024]{1,0:T(8,128)(2,1)S(1)}, u32[]{:S(2)}, u32[]{:S(2)}) collective-permute-start(bf16[144,1024]{1,0:T(8,128)(2,1)} %dynamic-slice_bitcast_fusion.1), channel_id=1, source_target_pairs={{0,8},{8,0},{1,9},{9,1},{2,10},{10,2},{3,11},{11,3},{4,12},{12,4},... | collective-permute-start | bytes 884744 | tf_op jit(solution)/shard_map/ppermute | solution.py:274
  128.9 5.9 %collective-permute-start.22 = (bf16[8,8,2048]{2,1,0:T(8,128)(2,1)S(1)}, bf16[8,8,2048]{2,1,0:T(8,128)(2,1)S(1)}, u32[]{:S(2)}, u32[]{:S(2)}) collective-permute-start(bf16[8,8,2048]{2,1,0:T(8,128)(2,1)S(1)} %bitcast.221), channel_id=1, source_target_pairs={{0,16},{16,32},{32,48},{48,64},{64,80},{80,96},{96,112},{112,0},{1... | collective-permute-start | bytes 786440 | tf_op jit(solution)/shard_map/ppermute | solution.py:288
  134.8 6.3 %collective-permute-done.20 = bf16[8,8,2048]{2,1,0:T(8,128)(2,1)S(1)} collective-permute-done((bf16[8,8,2048]{2,1,0:T(8,128)(2,1)S(1)}, bf16[8,8,2048]{2,1,0:T(8,128)(2,1)S(1)}, u32[]{:S(2)}, u32[]{:S(2)}) %collective-permute-start.20) | collective-permute-done | bytes 262176 | tf_op jit(solution)/shard_map/ppermute | solution.py:289
  144.0 5.2 %collective-permute-done.23 = bf16[8,8,2048]{2,1,0:T(8,128)(2,1)S(1)} collective-permute-done((bf16[8,8,2048]{2,1,0:T(8,128)(2,1)S(1)}, bf16[8,8,2048]{2,1,0:T(8,128)(2,1)S(1)}, u32[]{:S(2)}, u32[]{:S(2)}) %collective-permute-start.23) | collective-permute-done | bytes 262176 | tf_op jit(solution)/shard_map/ppermute | solution.py:288
  149.2 2.7 %collective-permute-start.24 = (bf16[8,8,2048]{2,1,0:T(8,128)(2,1)S(1)}, bf16[8,8,2048]{2,1,0:T(8,128)(2,1)S(1)}, u32[]{:S(2)}, u32[]{:S(2)}) collective-permute-start(bf16[8,8,2048]{2,1,0:T(8,128)(2,1)S(1)} %collective-permute-done.21), channel_id=1, source_target_pairs={{0,112},{16,0},{32,16},{48,32},{64,48},{80,64},{96,80},{112,96},{1... | collective-permute-start | bytes 786440 | tf_op jit(solution)/shard_map/ppermute | solution.py:289
  151.9 3.5 %collective-permute-done.24 = bf16[8,8,2048]{2,1,0:T(8,128)(2,1)S(1)} collective-permute-done((bf16[8,8,2048]{2,1,0:T(8,128)(2,1)S(1)}, bf16[8,8,2048]{2,1,0:T(8,128)(2,1)S(1)}, u32[]{:S(2)}, u32[]{:S(2)}) %collective-permute-start.24) | collective-permute-done | bytes 262176 | tf_op jit(solution)/shard_map/ppermute | solution.py:289
  155.4 3.5 %collective-permute-start.27 = (bf16[4,8,2048]{2,1,0:T(8,128)(2,1)S(1)}, bf16[4,8,2048]{2,1,0:T(8,128)(2,1)S(1)}, u32[]{:S(2)}, u32[]{:S(2)}) collective-permute-start(bf16[4,8,2048]{2,1,0:T(8,128)(2,1)S(1)} %slice.89), channel_id=1, source_target_pairs={{0,112},{16,0},{32,16},{48,32},{64,48},{80,64},{96,80},{112,96},{1... | collective-permute-start | bytes 393224 | tf_op jit(solution)/shard_map/ppermute | solution.py:298
  159.2 1.7 collective-permute-done.27
  160.9 3.2 %collective-permute-done.26 = bf16[4,8,2048]{2,1,0:T(8,128)(2,1)S(1)} collective-permute-done((bf16[4,8,2048]{2,1,0:T(8,128)(2,1)S(1)}, bf16[4,8,2048]{2,1,0:T(8,128)(2,1)S(1)}, u32[]{:S(2)}, u32[]{:S(2)}) %collective-permute-start.26) | collective-permute-done | bytes 131104 | tf_op jit(solution)/shard_map/ppermute | solution.py:297
  164.3 2.5 %select_bitcast_fusion.3 = (bf16[1,2048,512]{2,1,0:T(8,128)(2,1)S(1)}, bf16[1,2048,512]{2,1,0:T(8,128)(2,1)S(1)}, bf16[1,2048,512]{2,1,0:T(8,128)(2,1)S(1)}, bf16[1,2048,512]{2,1,0:T(8,128)(2,1)S(1)}) fusion(pred[]{:T(512)S(6)} %eq.90, bf16[2048,512]{1,0:T(8,128)(2,1)S(1)} %copy-done, bf16[2048,512]{1,0:T(8,128)(2,1)} %collective-permute-done, pred[]{:T(512)S(6)} %eq.91, ...), kind=kLoop, calls=%fused_computation.4 | loop fusion | flops 8388608 | bytes 16777218 | tf_op jit(solution)/shard_map/stack | solution.py:226
  166.9 3.9 %fusion.1 = bf16[4,512,192]{1,2,0:T(8,128)(2,1)} fusion(bf16[192,2048,1]{1,0,2:T(8,128)(2,1)S(1)} %bitcast.234, bf16[1,2048,512]{2,1,0:T(8,128)(2,1)S(1)} %get-tuple-element.30, bf16[1,2048,512]{2,1,0:T(8,128)(2,1)S(1)} %get-tuple-element.29, bf16[1,2048,512]{2,1,0:T(8,128)(2,1)S(1)} %get-tuple-element.28, bf16[1,2048,512]{2,1,0:T(8,128)(2,1)S(1)} %get-tuple-element.27), kind=kOutput, calls=%fused_computation.11 | convolution fusion | flops 1644560384 | bytes 9961472 | tf_op jit(solution)/shard_map/rk,wkn->wrn/dot_general | solution.py:306
  170.8 11.2 %all-to-all-start.2 = ((bf16[32,24,512]{2,1,0:T(8,128)(2,1)}), bf16[32,24,512]{2,1,0:T(8,128)(2,1)S(1)}, u32[]{:S(2)}, u32[]{:S(2)}) async-start(bf16[32,24,512]{2,1,0:T(8,128)(2,1)} %bitcast.100), calls=%async_computation.2 | async-start | bytes 1572864 | tf_op jit(solution)/shard_map/all_to_all | solution.py:308
  182.1 6.1 %convolution_convert_fusion = bf16[4,512,320]{1,2,0:T(8,128)(2,1)} fusion(bf16[320,2048,1]{1,0,2:T(8,128)(2,1)S(1)} %bitcast.232, bf16[1,2048,512]{2,1,0:T(8,128)(2,1)} %copy-done.4, bf16[1,2048,512]{2,1,0:T(8,128)(2,1)} %copy-done.3, bf16[1,2048,512]{2,1,0:T(8,128)(2,1)} %copy-done.2, bf16[1,2048,512]{2,1,0:T(8,128)(2,1)} %copy-done.1), kind=kOutput, calls=%fused_computation.9 | convolution fusion | flops 2718564352 | bytes 11010048 | tf_op jit(solution)/shard_map/rk,wkn->wrn/dot_general | solution.py:306
  188.2 8.6 %all-to-all-done.2 = bf16[32,24,512]{2,1,0:T(8,128)(2,1)S(1)} async-done(((bf16[32,24,512]{2,1,0:T(8,128)(2,1)}), bf16[32,24,512]{2,1,0:T(8,128)(2,1)S(1)}, u32[]{:S(2)}, u32[]{:S(2)}) %all-to-all-start.2) | async-done | bytes 786464 | tf_op jit(solution)/shard_map/all_to_all | solution.py:308
  196.8 3.7 %all-to-all-start.1 = ((bf16[32,40,512]{2,1,0:T(8,128)(2,1)}), bf16[32,40,512]{2,1,0:T(8,128)(2,1)S(1)}, u32[]{:S(2)}, u32[]{:S(2)}) async-start(bf16[32,40,512]{2,1,0:T(8,128)(2,1)} %bitcast.89), calls=%async_computation.1 | async-start | bytes 2621440 | tf_op jit(solution)/shard_map/all_to_all | solution.py:308
  200.7 20.2 %all-to-all-done.1 = bf16[32,40,512]{2,1,0:T(8,128)(2,1)S(1)} async-done(((bf16[32,40,512]{2,1,0:T(8,128)(2,1)}), bf16[32,40,512]{2,1,0:T(8,128)(2,1)S(1)}, u32[]{:S(2)}, u32[]{:S(2)}) %all-to-all-start.1) | async-done | bytes 1310752 | tf_op jit(solution)/shard_map/all_to_all | solution.py:308
  (165 shorter events, 28.4 us)
Async XLA Ops:
  0.0 12.9 %copy-start.5 = (bf16[1,16,1,256,128]{4,3,2,1,0:T(8,128)(2,1)S(1)}, bf16[1,16,1,256,128]{4,3,2,1,0:T(8,128)(2,1)}, u32[]{:S(2)}) copy-start(bf16[1,16,1,256,128]{4,3,2,1,0:T(8,128)(2,1)} %param.13) | copy-start | bytes 3145732
  2.6 38.8 %all-to-all-start = ((bf16[16,80,128]{2,1,0:T(8,128)(2,1)}), bf16[16,80,128]{2,1,0:T(8,128)(2,1)S(1)}, u32[]{:S(2)}, u32[]{:S(2)}) async-start(bf16[16,80,128]{2,1,0:T(8,128)(2,1)} %pad_maximum_fusion.7), calls=%async_computation | async-start | bytes 655360 | tf_op jit(solution)/shard_map/all_to_all | solution.py:190
  12.9 11.2 %copy-start.19 = (s32[16]{0:T(128)S(1)}, s32[16]{0:T(128)}, u32[]{:S(2)}) copy-start(s32[16]{0:T(128)} %param.15) | copy-start | bytes 196
  15.7 22.9 %copy-start.10 = (bf16[256,128]{1,0:T(8,128)(2,1)S(1)}, bf16[256,128]{1,0:T(8,128)(2,1)}, u32[]{:S(2)}) copy-start(bf16[256,128]{1,0:T(8,128)(2,1)} %get-tuple-element.54) | copy-start | bytes 196612
  15.7 24.3 %copy-start.8 = (bf16[256,128]{1,0:T(8,128)(2,1)S(1)}, bf16[256,128]{1,0:T(8,128)(2,1)}, u32[]{:S(2)}) copy-start(bf16[256,128]{1,0:T(8,128)(2,1)} %get-tuple-element.53) | copy-start | bytes 196612
  15.7 24.3 %copy-start.9 = (bf16[256,128]{1,0:T(8,128)(2,1)S(1)}, bf16[256,128]{1,0:T(8,128)(2,1)}, u32[]{:S(2)}) copy-start(bf16[256,128]{1,0:T(8,128)(2,1)} %get-tuple-element.100) | copy-start | bytes 196612
  15.7 25.6 %copy-start.6 = (bf16[256,128]{1,0:T(8,128)(2,1)S(1)}, bf16[256,128]{1,0:T(8,128)(2,1)}, u32[]{:S(2)}) copy-start(bf16[256,128]{1,0:T(8,128)(2,1)} %get-tuple-element.49) | copy-start | bytes 196612
  15.8 25.6 %copy-start.7 = (bf16[256,128]{1,0:T(8,128)(2,1)S(1)}, bf16[256,128]{1,0:T(8,128)(2,1)}, u32[]{:S(2)}) copy-start(bf16[256,128]{1,0:T(8,128)(2,1)} %get-tuple-element.104) | copy-start | bytes 196612
  16.4 59.7 %collective-permute-start.12 = (bf16[512,128]{1,0:T(8,128)(2,1)}, bf16[512,128]{1,0:T(8,128)(2,1)S(1)}, u32[]{:S(2)}, u32[]{:S(2)}) collective-permute-start(bf16[512,128]{1,0:T(8,128)(2,1)} %pad_maximum_fusion.16), channel_id=1, source_target_pairs={{0,144},{16,160},{32,176},{48,192},{64,208},{80,224},{96,240},{112... | collective-permute-start | bytes 393224 | tf_op jit(solution)/shard_map/ppermute | solution.py:211
  19.1 35.0 %copy-start = (bf16[2048,512]{1,0:T(8,128)(2,1)S(1)}, bf16[2048,512]{1,0:T(8,128)(2,1)}, u32[]{:S(2)}) copy-start(bf16[2048,512]{1,0:T(8,128)(2,1)} %param.17) | copy-start | bytes 6291460
  19.1 47.4 %collective-permute-start.16 = (bf16[512,128]{1,0:T(8,128)(2,1)}, bf16[512,128]{1,0:T(8,128)(2,1)S(1)}, u32[]{:S(2)}, u32[]{:S(2)}) collective-permute-start(bf16[512,128]{1,0:T(8,128)(2,1)} %pad_maximum_fusion.20), channel_id=1, source_target_pairs={{0,128},{16,144},{32,160},{48,176},{64,192},{80,208},{96,224},{112... | collective-permute-start | bytes 393224 | tf_op jit(solution)/shard_map/ppermute | solution.py:211
  20.1 46.5 %collective-permute-start.17 = (bf16[512,128]{1,0:T(8,128)(2,1)}, bf16[512,128]{1,0:T(8,128)(2,1)S(1)}, u32[]{:S(2)}, u32[]{:S(2)}) collective-permute-start(bf16[512,128]{1,0:T(8,128)(2,1)} %pad_maximum_fusion.21), channel_id=1, source_target_pairs={{0,16},{16,32},{32,48},{48,64},{64,80},{80,96},{96,112},{112,0},{1... | collective-permute-start | bytes 393224 | tf_op jit(solution)/shard_map/ppermute | solution.py:211
  21.9 46.3 %collective-permute-start.18 = (bf16[512,128]{1,0:T(8,128)(2,1)}, bf16[512,128]{1,0:T(8,128)(2,1)S(1)}, u32[]{:S(2)}, u32[]{:S(2)}) collective-permute-start(bf16[512,128]{1,0:T(8,128)(2,1)} %pad_maximum_fusion.22), channel_id=1, source_target_pairs={{0,112},{16,0},{32,16},{48,32},{64,48},{80,64},{96,80},{112,96},{1... | collective-permute-start | bytes 393224 | tf_op jit(solution)/shard_map/ppermute | solution.py:211
  44.1 10.0 %collective-permute-start.3 = (bf16[16,80,128]{2,1,0:T(8,128)(2,1)S(1)}, bf16[16,80,128]{2,1,0:T(8,128)(2,1)S(1)}, u32[]{:S(2)}, u32[]{:S(2)}) collective-permute-start(bf16[16,80,128]{2,1,0:T(8,128)(2,1)S(1)} %all-to-all-done), channel_id=1, source_target_pairs={{0,8},{8,0},{1,9},{9,1},{2,10},{10,2},{3,11},{11,3},{4,12},{12,4},... | collective-permute-start | bytes 983048 | tf_op jit(solution)/shard_map/ppermute | solution.py:191
  54.2 88.4 %collective-permute-start.1 = (bf16[2048,512]{1,0:T(8,128)(2,1)S(1)}, bf16[2048,512]{1,0:T(8,128)(2,1)}, u32[]{:S(2)}, u32[]{:S(2)}) collective-permute-start(bf16[2048,512]{1,0:T(8,128)(2,1)S(1)} %copy-done), channel_id=1, source_target_pairs={{0,128},{128,0},{1,129},{129,1},{2,130},{130,2},{3,131},{131,3},{4... | collective-permute-start | bytes 6291464 | tf_op jit(solution)/shard_map/ppermute | solution.py:216
  66.5 12.8 %collective-permute-start.13 = (bf16[512,128]{1,0:T(8,128)(2,1)}, bf16[512,128]{1,0:T(8,128)(2,1)S(1)}, u32[]{:S(2)}, u32[]{:S(2)}) collective-permute-start(bf16[512,128]{1,0:T(8,128)(2,1)} %pad_maximum_fusion.17), channel_id=1, source_target_pairs={{0,240},{16,128},{32,144},{48,160},{64,176},{80,192},{96,208},{112... | collective-permute-start | bytes 393224 | tf_op jit(solution)/shard_map/ppermute | solution.py:211
  66.6 14.3 %collective-permute-start.14 = (bf16[512,128]{1,0:T(8,128)(2,1)}, bf16[512,128]{1,0:T(8,128)(2,1)S(1)}, u32[]{:S(2)}, u32[]{:S(2)}) collective-permute-start(bf16[512,128]{1,0:T(8,128)(2,1)} %pad_maximum_fusion.18), channel_id=1, source_target_pairs={{0,32},{16,48},{32,64},{48,80},{64,96},{80,112},{96,0},{112,16},{1... | collective-permute-start | bytes 393224 | tf_op jit(solution)/shard_map/ppermute | solution.py:211
  68.2 14.8 %collective-permute-start.15 = (bf16[512,128]{1,0:T(8,128)(2,1)}, bf16[512,128]{1,0:T(8,128)(2,1)S(1)}, u32[]{:S(2)}, u32[]{:S(2)}) collective-permute-start(bf16[512,128]{1,0:T(8,128)(2,1)} %pad_maximum_fusion.19), channel_id=1, source_target_pairs={{0,96},{16,112},{32,0},{48,16},{64,32},{80,48},{96,64},{112,80},{1... | collective-permute-start | bytes 393224 | tf_op jit(solution)/shard_map/ppermute | solution.py:211
  70.3 5.9 %copy-start.17 = (bf16[512,128]{1,0:T(8,128)(2,1)S(1)}, bf16[512,128]{1,0:T(8,128)(2,1)}, u32[]{:S(2)}) copy-start(bf16[512,128]{1,0:T(8,128)(2,1)} %pad_maximum_fusion.12) | copy-start | bytes 393220
  70.3 9.0 %copy-start.16 = (bf16[512,128]{1,0:T(8,128)(2,1)S(1)}, bf16[512,128]{1,0:T(8,128)(2,1)}, u32[]{:S(2)}) copy-start(bf16[512,128]{1,0:T(8,128)(2,1)} %pad_maximum_fusion.13) | copy-start | bytes 393220
  70.3 10.6 %copy-start.15 = (bf16[512,128]{1,0:T(8,128)(2,1)S(1)}, bf16[512,128]{1,0:T(8,128)(2,1)}, u32[]{:S(2)}) copy-start(bf16[512,128]{1,0:T(8,128)(2,1)} %pad_maximum_fusion.14) | copy-start | bytes 393220
  70.3 12.7 %copy-start.18 = (bf16[512,128]{1,0:T(8,128)(2,1)S(1)}, bf16[512,128]{1,0:T(8,128)(2,1)}, u32[]{:S(2)}) copy-start(bf16[512,128]{1,0:T(8,128)(2,1)} %pad_maximum_fusion.15) | copy-start | bytes 393220
  76.1 16.4 %collective-permute-start.8 = (bf16[512,128]{1,0:T(8,128)(2,1)S(1)}, bf16[512,128]{1,0:T(8,128)(2,1)S(1)}, u32[]{:S(2)}, u32[]{:S(2)}) collective-permute-start(bf16[512,128]{1,0:T(8,128)(2,1)S(1)} %copy-done.17), channel_id=1, source_target_pairs={{0,160},{16,176},{32,192},{48,208},{64,224},{80,240},{96,128},{112... | collective-permute-start | bytes 393224 | tf_op jit(solution)/shard_map/ppermute | solution.py:211
  79.3 14.2 %collective-permute-start.9 = (bf16[512,128]{1,0:T(8,128)(2,1)S(1)}, bf16[512,128]{1,0:T(8,128)(2,1)S(1)}, u32[]{:S(2)}, u32[]{:S(2)}) collective-permute-start(bf16[512,128]{1,0:T(8,128)(2,1)S(1)} %copy-done.16), channel_id=1, source_target_pairs={{0,224},{16,240},{32,128},{48,144},{64,160},{80,176},{96,192},{112... | collective-permute-start | bytes 393224 | tf_op jit(solution)/shard_map/ppermute | solution.py:211
  80.9 17.2 %collective-permute-start.10 = (bf16[512,128]{1,0:T(8,128)(2,1)S(1)}, bf16[512,128]{1,0:T(8,128)(2,1)S(1)}, u32[]{:S(2)}, u32[]{:S(2)}) collective-permute-start(bf16[512,128]{1,0:T(8,128)(2,1)S(1)} %copy-done.15), channel_id=1, source_target_pairs={{0,48},{16,64},{32,80},{48,96},{64,112},{80,0},{96,16},{112,32},{1... | collective-permute-start | bytes 393224 | tf_op jit(solution)/shard_map/ppermute | solution.py:211
  83.0 20.3 %collective-permute-start.11 = (bf16[512,128]{1,0:T(8,128)(2,1)S(1)}, bf16[512,128]{1,0:T(8,128)(2,1)S(1)}, u32[]{:S(2)}, u32[]{:S(2)}) collective-permute-start(bf16[512,128]{1,0:T(8,128)(2,1)S(1)} %copy-done.18), channel_id=1, source_target_pairs={{0,80},{16,96},{32,112},{48,0},{64,16},{80,32},{96,48},{112,64},{1... | collective-permute-start | bytes 393224 | tf_op jit(solution)/shard_map/ppermute | solution.py:211
  85.4 7.2 %copy-start.14 = (bf16[512,128]{1,0:T(8,128)(2,1)S(1)}, bf16[512,128]{1,0:T(8,128)(2,1)}, u32[]{:S(2)}) copy-start(bf16[512,128]{1,0:T(8,128)(2,1)} %pad_maximum_fusion.8) | copy-start | bytes 393220
  85.4 8.2 %copy-start.13 = (bf16[512,128]{1,0:T(8,128)(2,1)S(1)}, bf16[512,128]{1,0:T(8,128)(2,1)}, u32[]{:S(2)}) copy-start(bf16[512,128]{1,0:T(8,128)(2,1)} %pad_maximum_fusion.9) | copy-start | bytes 393220
  85.4 12.7 %copy-start.12 = (bf16[512,128]{1,0:T(8,128)(2,1)S(1)}, bf16[512,128]{1,0:T(8,128)(2,1)}, u32[]{:S(2)}) copy-start(bf16[512,128]{1,0:T(8,128)(2,1)} %pad_maximum_fusion.10) | copy-start | bytes 393220
  85.4 17.9 %copy-start.11 = (bf16[512,128]{1,0:T(8,128)(2,1)S(1)}, bf16[512,128]{1,0:T(8,128)(2,1)}, u32[]{:S(2)}) copy-start(bf16[512,128]{1,0:T(8,128)(2,1)} %pad_maximum_fusion.11) | copy-start | bytes 393220
  92.6 19.1 %collective-permute-start.4 = (bf16[512,128]{1,0:T(8,128)(2,1)S(1)}, bf16[512,128]{1,0:T(8,128)(2,1)S(1)}, u32[]{:S(2)}, u32[]{:S(2)}) collective-permute-start(bf16[512,128]{1,0:T(8,128)(2,1)S(1)} %copy-done.14), channel_id=1, source_target_pairs={{0,176},{16,192},{32,208},{48,224},{64,240},{80,128},{96,144},{112... | collective-permute-start | bytes 393224 | tf_op jit(solution)/shard_map/ppermute | solution.py:211
  93.5 21.6 %collective-permute-start.5 = (bf16[512,128]{1,0:T(8,128)(2,1)S(1)}, bf16[512,128]{1,0:T(8,128)(2,1)S(1)}, u32[]{:S(2)}, u32[]{:S(2)}) collective-permute-start(bf16[512,128]{1,0:T(8,128)(2,1)S(1)} %copy-done.13), channel_id=1, source_target_pairs={{0,208},{16,224},{32,240},{48,128},{64,144},{80,160},{96,176},{112... | collective-permute-start | bytes 393224 | tf_op jit(solution)/shard_map/ppermute | solution.py:211
  98.1 17.1 %collective-permute-start.6 = (bf16[512,128]{1,0:T(8,128)(2,1)S(1)}, bf16[512,128]{1,0:T(8,128)(2,1)S(1)}, u32[]{:S(2)}, u32[]{:S(2)}) collective-permute-start(bf16[512,128]{1,0:T(8,128)(2,1)S(1)} %copy-done.12), channel_id=1, source_target_pairs={{0,64},{16,80},{32,96},{48,112},{64,0},{80,16},{96,32},{112,48},{1... | collective-permute-start | bytes 393224 | tf_op jit(solution)/shard_map/ppermute | solution.py:211
  103.3 11.8 %collective-permute-start.7 = (bf16[512,128]{1,0:T(8,128)(2,1)S(1)}, bf16[512,128]{1,0:T(8,128)(2,1)S(1)}, u32[]{:S(2)}, u32[]{:S(2)}) collective-permute-start(bf16[512,128]{1,0:T(8,128)(2,1)S(1)} %copy-done.11), channel_id=1, source_target_pairs={{0,192},{16,208},{32,224},{48,240},{64,128},{80,144},{96,160},{112... | collective-permute-start | bytes 393224 | tf_op jit(solution)/shard_map/ppermute | solution.py:211
  111.7 52.6 %collective-permute-start = (bf16[2048,512]{1,0:T(8,128)(2,1)S(1)}, bf16[2048,512]{1,0:T(8,128)(2,1)}, u32[]{:S(2)}, u32[]{:S(2)}) collective-permute-start(bf16[2048,512]{1,0:T(8,128)(2,1)S(1)} %copy-done), channel_id=1, source_target_pairs={{0,8},{8,0},{1,9},{9,1},{2,10},{10,2},{3,11},{11,3},{4,12},{12,4},... | collective-permute-start | bytes 6291464 | tf_op jit(solution)/shard_map/ppermute | solution.py:215
  123.3 5.4 %collective-permute-start.19 = (bf16[144,1024]{1,0:T(8,128)(2,1)}, bf16[144,1024]{1,0:T(8,128)(2,1)S(1)}, u32[]{:S(2)}, u32[]{:S(2)}) collective-permute-start(bf16[144,1024]{1,0:T(8,128)(2,1)} %dynamic-slice_bitcast_fusion.1), channel_id=1, source_target_pairs={{0,8},{8,0},{1,9},{9,1},{2,10},{10,2},{3,11},{11,3},{4,12},{12,4},... | collective-permute-start | bytes 884744 | tf_op jit(solution)/shard_map/ppermute | solution.py:274
  128.8 12.2 %collective-permute-start.20 = (bf16[8,8,2048]{2,1,0:T(8,128)(2,1)S(1)}, bf16[8,8,2048]{2,1,0:T(8,128)(2,1)S(1)}, u32[]{:S(2)}, u32[]{:S(2)}) collective-permute-start(bf16[8,8,2048]{2,1,0:T(8,128)(2,1)S(1)} %bitcast.220), channel_id=1, source_target_pairs={{0,112},{16,0},{32,16},{48,32},{64,48},{80,64},{96,80},{112,96},{1... | collective-permute-start | bytes 786440 | tf_op jit(solution)/shard_map/ppermute | solution.py:289
  128.9 12.2 %collective-permute-start.22 = (bf16[8,8,2048]{2,1,0:T(8,128)(2,1)S(1)}, bf16[8,8,2048]{2,1,0:T(8,128)(2,1)S(1)}, u32[]{:S(2)}, u32[]{:S(2)}) collective-permute-start(bf16[8,8,2048]{2,1,0:T(8,128)(2,1)S(1)} %bitcast.221), channel_id=1, source_target_pairs={{0,16},{16,32},{32,48},{48,64},{64,80},{80,96},{96,112},{112,0},{1... | collective-permute-start | bytes 786440 | tf_op jit(solution)/shard_map/ppermute | solution.py:288
  141.1 8.2 %collective-permute-start.21 = (bf16[8,8,2048]{2,1,0:T(8,128)(2,1)S(1)}, bf16[8,8,2048]{2,1,0:T(8,128)(2,1)S(1)}, u32[]{:S(2)}, u32[]{:S(2)}) collective-permute-start(bf16[8,8,2048]{2,1,0:T(8,128)(2,1)S(1)} %collective-permute-done.20), channel_id=1, source_target_pairs={{0,112},{16,0},{32,16},{48,32},{64,48},{80,64},{96,80},{112,96},{1... | collective-permute-start | bytes 786440 | tf_op jit(solution)/shard_map/ppermute | solution.py:289
  141.1 8.2 %collective-permute-start.23 = (bf16[8,8,2048]{2,1,0:T(8,128)(2,1)S(1)}, bf16[8,8,2048]{2,1,0:T(8,128)(2,1)S(1)}, u32[]{:S(2)}, u32[]{:S(2)}) collective-permute-start(bf16[8,8,2048]{2,1,0:T(8,128)(2,1)S(1)} %collective-permute-done.22), channel_id=1, source_target_pairs={{0,16},{16,32},{32,48},{48,64},{64,80},{80,96},{96,112},{112,0},{1... | collective-permute-start | bytes 786440 | tf_op jit(solution)/shard_map/ppermute | solution.py:288
  142.5 21.7 %collective-permute-start.2 = (bf16[2048,512]{1,0:T(8,128)(2,1)}, bf16[2048,512]{1,0:T(8,128)(2,1)S(1)}, u32[]{:S(2)}, u32[]{:S(2)}) collective-permute-start(bf16[2048,512]{1,0:T(8,128)(2,1)} %collective-permute-done.1), channel_id=1, source_target_pairs={{0,8},{8,0},{1,9},{9,1},{2,10},{10,2},{3,11},{11,3},{4,12},{12,4},... | collective-permute-start | bytes 6291464 | tf_op jit(solution)/shard_map/ppermute | solution.py:217
  149.2 9.7 %collective-permute-start.25 = (bf16[8,8,2048]{2,1,0:T(8,128)(2,1)S(1)}, bf16[8,8,2048]{2,1,0:T(8,128)(2,1)S(1)}, u32[]{:S(2)}, u32[]{:S(2)}) collective-permute-start(bf16[8,8,2048]{2,1,0:T(8,128)(2,1)S(1)} %collective-permute-done.23), channel_id=1, source_target_pairs={{0,16},{16,32},{32,48},{48,64},{64,80},{80,96},{96,112},{112,0},{1... | collective-permute-start | bytes 786440 | tf_op jit(solution)/shard_map/ppermute | solution.py:288
  149.2 6.2 %collective-permute-start.24 = (bf16[8,8,2048]{2,1,0:T(8,128)(2,1)S(1)}, bf16[8,8,2048]{2,1,0:T(8,128)(2,1)S(1)}, u32[]{:S(2)}, u32[]{:S(2)}) collective-permute-start(bf16[8,8,2048]{2,1,0:T(8,128)(2,1)S(1)} %collective-permute-done.21), channel_id=1, source_target_pairs={{0,112},{16,0},{32,16},{48,32},{64,48},{80,64},{96,80},{112,96},{1... | collective-permute-start | bytes 786440 | tf_op jit(solution)/shard_map/ppermute | solution.py:289
  155.4 5.4 %collective-permute-start.27 = (bf16[4,8,2048]{2,1,0:T(8,128)(2,1)S(1)}, bf16[4,8,2048]{2,1,0:T(8,128)(2,1)S(1)}, u32[]{:S(2)}, u32[]{:S(2)}) collective-permute-start(bf16[4,8,2048]{2,1,0:T(8,128)(2,1)S(1)} %slice.89), channel_id=1, source_target_pairs={{0,112},{16,0},{32,16},{48,32},{64,48},{80,64},{96,80},{112,96},{1... | collective-permute-start | bytes 393224 | tf_op jit(solution)/shard_map/ppermute | solution.py:298
  159.0 5.1 %collective-permute-start.26 = (bf16[4,8,2048]{2,1,0:T(8,128)(2,1)S(1)}, bf16[4,8,2048]{2,1,0:T(8,128)(2,1)S(1)}, u32[]{:S(2)}, u32[]{:S(2)}) collective-permute-start(bf16[4,8,2048]{2,1,0:T(8,128)(2,1)S(1)} %slice.88), channel_id=1, source_target_pairs={{0,16},{16,32},{32,48},{48,64},{64,80},{80,96},{96,112},{112,0},{1... | collective-permute-start | bytes 393224 | tf_op jit(solution)/shard_map/ppermute | solution.py:297
  166.8 4.0 %copy-start.1 = (bf16[1,2048,512]{2,1,0:T(8,128)(2,1)}, bf16[1,2048,512]{2,1,0:T(8,128)(2,1)S(1)}, u32[]{:S(2)}) copy-start(bf16[1,2048,512]{2,1,0:T(8,128)(2,1)S(1)} %get-tuple-element.27) | copy-start | bytes 6291460
  170.8 26.0 %all-to-all-start.2 = ((bf16[32,24,512]{2,1,0:T(8,128)(2,1)}), bf16[32,24,512]{2,1,0:T(8,128)(2,1)S(1)}, u32[]{:S(2)}, u32[]{:S(2)}) async-start(bf16[32,24,512]{2,1,0:T(8,128)(2,1)} %bitcast.100), calls=%async_computation.2 | async-start | bytes 1572864 | tf_op jit(solution)/shard_map/all_to_all | solution.py:308
  196.8 24.1 %all-to-all-start.1 = ((bf16[32,40,512]{2,1,0:T(8,128)(2,1)}), bf16[32,40,512]{2,1,0:T(8,128)(2,1)S(1)}, u32[]{:S(2)}, u32[]{:S(2)}) async-start(bf16[32,40,512]{2,1,0:T(8,128)(2,1)} %bitcast.89), calls=%async_computation.1 | async-start | bytes 2621440 | tf_op jit(solution)/shard_map/all_to_all | solution.py:308
  (3 other events, 11.9 us)

commit v2 on v1

v2 whole, which is shorter than its diff:
```python
import functools

import jax
import jax.numpy as jnp
from jax import lax
from jax.experimental import pallas as pl
from jax.experimental.pallas import tpu as pltpu
from jax.sharding import Mesh, PartitionSpec as P

LOG2_E = 1.4426950408889634
ROWS = 256
SHARDS_AT_ONCE = 4
CLOSED = 1.0e9
SHUT = -1.0e30


def attend_kernel(
    as_message, lens_ref, q_ref, kv_ref, new_k_ref, new_v_ref, key_index_ref, row_index_ref, *refs
):
    keys_ref, values_ref = refs[-2:]
    outs = refs[:-2]
    shards, slots, width = kv_ref.shape[0], kv_ref.shape[1] // 2, kv_ref.shape[2]
    scale = LOG2_E / width**0.5
    first_lane = lax.broadcasted_iota(jnp.int32, (slots, width), 1) == 0
    slot = lax.broadcasted_iota(jnp.int32, (slots, width), 0)
    for i in range(shards):
        keys_ref[i, :, 0:width] = kv_ref[i, 0:slots, :]
        shut = first_lane & (slot >= lens_ref[i])
        keys_ref[i, :, width : 2 * width] = jnp.where(shut, SHUT, 0.0).astype(jnp.bfloat16)
        values_ref[i, :, 0:width] = kv_ref[i, slots : 2 * slots, :]
        values_ref[i, :, width : 2 * width] = jnp.ones((slots, width), jnp.bfloat16)
    lane = lax.broadcasted_iota(jnp.int32, (ROWS, width), 1)
    unit = jnp.where(lane == 0, 1.0, 0.0).astype(jnp.bfloat16)
    ones = jnp.ones((new_v_ref.shape[0], width), jnp.bfloat16)
    seen = key_index_ref[0:1, :] <= row_index_ref[...]
    new_v = jnp.concatenate([new_v_ref[...], ones], 1)

    def score(a, b):
        return lax.dot_general(a, b, (((1,), (1,)), ((), ())), preferred_element_type=jnp.float32)

    def rows_step(block, carry):
        at = pl.ds(pl.multiple_of(block * ROWS, ROWS), ROWS)
        q = q_ref[at, :]
        wide = jnp.concatenate([q, unit], 1)
        new_s = jnp.where(seen, score(q, new_k_ref[...]), SHUT)
        top = jnp.max(new_s, axis=1, keepdims=True)
        sums = None
        for start in range(0, shards, SHARDS_AT_ONCE):
            some = slice(start, start + SHARDS_AT_ONCE)
            s = score(wide, keys_ref[some].reshape(SHARDS_AT_ONCE * slots, 2 * width))
            raised = jnp.maximum(top, jnp.max(s, axis=1, keepdims=True))
            low = raised * scale
            if sums is None:
                w = jnp.exp2(new_s * scale - low).astype(jnp.bfloat16)
                sums = jnp.dot(w, new_v, preferred_element_type=jnp.float32)
            else:
                sums = sums * jnp.exp2(top * scale - low)
            w = jnp.exp2(s * scale - low).astype(jnp.bfloat16)
            v = values_ref[some].reshape(SHARDS_AT_ONCE * slots, 2 * width)
            sums = sums + jnp.dot(w, v, preferred_element_type=jnp.float32)
            top = raised
        numerator, total = sums[:, 0:width], sums[:, width : 2 * width]
        if as_message:
            outs[0][at, 0:width] = numerator.astype(jnp.bfloat16)
            tail = jnp.zeros((ROWS, width), jnp.float32)
            for i, value in enumerate((jnp.broadcast_to(top, (ROWS, width)), total)):
                for j in range(3):
                    part = value.astype(jnp.bfloat16).astype(jnp.float32)
                    tail = jnp.where(lane == 3 * i + j, part, tail)
                    value = value - part
            outs[0][at, width : 2 * width] = tail.astype(jnp.bfloat16)
        else:
            outs[0][at, :] = numerator
            outs[1][at, :] = jnp.where(lane == 0, top, total)
        return carry

    lax.fori_loop(0, q_ref.shape[0] // ROWS, rows_step, 0)


def attend(as_message, lens, q, kv, new_k, new_v, key_index, row_index):
    rows, width = q.shape
    shards, slots = kv.shape[0], kv.shape[1] // 2
    if as_message:
        out_shape = [jax.ShapeDtypeStruct((rows, 2 * width), jnp.bfloat16)]
    else:
        out_shape = [jax.ShapeDtypeStruct((rows, width), jnp.float32)] * 2
    vmem = pl.BlockSpec(memory_space=pltpu.VMEM)
    wide = pltpu.VMEM((shards, slots, 2 * width), jnp.bfloat16)
    return pl.pallas_call(
        functools.partial(attend_kernel, as_message),
        in_specs=[pl.BlockSpec(memory_space=pltpu.SMEM)] + [vmem] * 6,
        out_specs=[vmem] * len(out_shape),
        out_shape=out_shape,
        scratch_shapes=[wide, wide],
        compiler_params=pltpu.CompilerParams(vmem_limit_bytes=40 * 1024 * 1024),
        cost_estimate=pl.CostEstimate(
            flops=8 * rows * width * shards * slots,
            bytes_accessed=4 * 1024 * 1024,
            transcendentals=rows * shards * slots,
        ),
    )(lens, q, kv, new_k, new_v, key_index, row_index)


def merge_kernel(sums_ref, stats_ref, message_ref, live_ref, out_ref):
    rows, width = sums_ref.shape
    tokens = out_ref.shape[0]
    scale = LOG2_E / width**0.5
    for head in range(rows // tokens):
        at = slice(head * tokens, (head + 1) * tokens)
        tail = message_ref[at, width : 2 * width].astype(jnp.float32)
        top_a, total_a = stats_ref[at, 0:1], stats_ref[at, 1:2]
        top_b = tail[:, 0:1] + tail[:, 1:2] + tail[:, 2:3]
        total_b = tail[:, 3:4] + tail[:, 4:5] + tail[:, 5:6]
        top = jnp.maximum(top_a, top_b)
        a = jnp.exp2((top_a - top) * scale)
        b = jnp.exp2((top_b - top) * scale)
        inverse = live_ref[:, 0:1] / (total_a * a + total_b * b)
        other = message_ref[at, 0:width].astype(jnp.float32)
        block = sums_ref[at, :] * (a * inverse) + other * (b * inverse)
        out_ref[:, head * width : (head + 1) * width] = block.astype(jnp.bfloat16)


def merge(sums, stats, message, live):
    rows, width = sums.shape
    tokens = live.shape[0]
    return pl.pallas_call(
        merge_kernel,
        out_shape=jax.ShapeDtypeStruct((tokens, rows // tokens * width), jnp.bfloat16),
        compiler_params=pltpu.CompilerParams(vmem_limit_bytes=40 * 1024 * 1024),
        cost_estimate=pl.CostEstimate(
            flops=4 * width * rows, bytes_accessed=14 * width * rows, transcendentals=2 * rows
        ),
    )(sums, stats, message, live)


def rotate(values, cosine, sine):
    half = values.shape[-1] // 2
    first, second = values[..., :half], values[..., half:]
    return jnp.concatenate(
        [first * cosine - second * sine, second * cosine + first * sine], -1
    ).astype(jnp.bfloat16)


def body(
    queries,
    unrotated_key_rows,
    incoming_value_rows,
    cache_keys,
    stored_value_rows,
    cache_len,
    new_count,
    slot_index,
    out_weight,
):
    ny, nz, nheads = lax.axis_size("y"), lax.axis_size("z"), lax.axis_size("head")
    y, z, core = lax.axis_index("y"), lax.axis_index("z"), lax.axis_index("core")
    convs, slots = slot_index.shape[1], slot_index.shape[2]
    shards = slot_index.shape[0]
    heads, width = queries.shape[1], queries.shape[2]
    here = y * nz + z
    other_core = [(0, 1), (1, 0)]

    kv = jnp.concatenate([cache_keys[0, :, 0], stored_value_rows[0, :, 0]], 1)
    kv = lax.all_to_all(kv, ("y", "z"), 0, 0, tiled=True)

    small = jnp.concatenate(
        [
            queries.reshape(convs, slots * heads, width),
            unrotated_key_rows.reshape(convs, slots, width),
            incoming_value_rows.reshape(convs, slots, width),
            jnp.broadcast_to(
                cache_len[0].astype(jnp.bfloat16)[:, None, None], (convs, 16 - 2 * slots, width)
            ),
        ],
        1,
    )

    def leg(dy, dz):
        target = (y - dy) % ny * nz + (z - dz) % nz
        block = lax.dynamic_index_in_dim(small, target, 0, keepdims=False)
        if (dy, dz) == (0, 0):
            return block
        route = [
            ((a + dy) % ny * nz + (b + dz) % nz, a * nz + b) for a in range(ny) for b in range(nz)
        ]
        return lax.ppermute(block, ("y", "z"), route)

    def unroll(values, axis, by):
        size = values.shape[axis]
        twice = jnp.concatenate([values, values], axis)
        return lax.dynamic_slice_in_dim(twice, (size - by) % size, size, axis)

    mine = jnp.stack([leg(dy, dz) for dy in range(ny) for dz in range(nz)])
    mine = mine.reshape((ny, nz) + small.shape[1:])
    theirs = lax.ppermute(mine, "core", other_core)

    weight, _ = lax.optimization_barrier((out_weight, theirs))
    weight_y = lax.ppermute(weight, "y", [(0, 1), (1, 0)])
    weight_core = lax.ppermute(weight, "core", other_core)
    weight_both = lax.ppermute(weight_y, "core", other_core)
    near = [
        jnp.where(core == 0, out_weight, weight_core),
        jnp.where(core == 0, weight_core, out_weight),
    ]
    far = [
        jnp.where(core == 0, weight_y, weight_both),
        jnp.where(core == 0, weight_both, weight_y),
    ]
    weights = jnp.stack(
        [jnp.where(y == 0, a, b) for a, b in zip(near, far)]
        + [jnp.where(y == 0, b, a) for a, b in zip(near, far)]
    )

    both = jnp.where(core == 0, jnp.stack([mine, theirs], 2), jnp.stack([theirs, mine], 2))
    both = unroll(unroll(both, 1, z), 0, y).reshape(shards, small.shape[1], width)
    lens = both[:, slots * heads + 2 * slots, 0]
    base = jnp.sum(lens.astype(jnp.float32))
    own_lens = lax.dynamic_index_in_dim(lens.reshape(shards // 2, 2), core, 1, keepdims=False)
    index = lax.dynamic_index_in_dim(slot_index, here, 1, keepdims=False)
    index = index.reshape(shards, 2, slots // 2).transpose(1, 0, 2)
    live = index < new_count[here]
    inverse = 1.0 / 500000.0 ** (jnp.arange(0, width, 2, dtype=jnp.float32) / width)
    angles = (base + index.astype(jnp.float32))[..., None] * inverse
    cosine, sine = jnp.cos(angles), jnp.sin(angles)
    q = both[:, : slots * heads].reshape(shards, 2, slots // 2, heads, width)
    q = q.transpose(1, 3, 0, 2, 4).astype(jnp.float32)
    q = rotate(q, cosine[:, None], sine[:, None])
    tokens = shards * slots // 2
    q = q.reshape(2, heads * tokens, width)

    def new_rows(start):
        rows = both[:, start : start + slots].reshape(shards, 2, slots // 2, width)
        return rows.transpose(1, 0, 2, 3)

    new_k = rotate(new_rows(slots * heads).astype(jnp.float32), cosine, sine)
    new_k = new_k.reshape(2 * tokens, width)
    new_v = new_rows(slots * heads + slots).reshape(2 * tokens, width)
    kept = live & (jnp.arange(shards)[None, :, None] % 2 == core)
    key_index = jnp.where(kept, index.astype(jnp.float32), CLOSED).reshape(1, 2 * tokens)
    key_index = jnp.broadcast_to(key_index, (8, 2 * tokens))
    row_index = jnp.broadcast_to(
        index.astype(jnp.float32).reshape(2, 1, tokens, 1), (2, ROWS // tokens, tokens, 128)
    ).reshape(2, ROWS, 128)

    def half(a, which):
        return lax.dynamic_index_in_dim(a, which, 0, keepdims=False)

    def attention(as_message, which):
        return attend(
            as_message,
            own_lens.astype(jnp.int32),
            half(q, which),
            kv,
            new_k,
            new_v,
            key_index,
            half(row_index, which),
        )

    (message,) = attention(True, 1 - core)
    message = lax.ppermute(message, "core", other_core)
    sums, stats = attention(False, core)
    live_rows = half(live, core).astype(jnp.float32).reshape(tokens, 1)
    attended = merge(sums, stats, message, jnp.broadcast_to(live_rows, (tokens, 128)))

    attended = attended.reshape(nheads, tokens // nheads, heads * width)
    up = [(i, (i + 1) % nz) for i in range(nz)]
    down = [(i, (i - 1) % nz) for i in range(nz)]
    held = {0: attended}
    for step in range(1, nz // 2):
        held[-step % nz] = lax.ppermute(held[(1 - step) % nz], "z", up)
        held[step] = lax.ppermute(held[step - 1], "z", down)
    def parts_of(which):
        rows = jnp.stack([held[k] for k in which], 1)
        rows = rows.reshape(-1, heads * width)
        parts = jnp.einsum("rk,wkn->wrn", rows, weights, preferred_element_type=jnp.float32)
        return parts.astype(jnp.bfloat16).reshape(4 * nheads, -1, out_weight.shape[1])

    def over_heads(parts, which):
        got = lax.all_to_all(parts, ("y", "core", "head"), 0, 0, tiled=True)
        got = got.reshape(ny, 2, nheads, len(which), tokens // nheads, -1)
        return jnp.sum(got.astype(jnp.float32), 2).astype(jnp.bfloat16)

    early = (0, 1, 2, nz - 2, nz - 1)
    late = tuple(range(3, nz - 2))
    early_parts = parts_of(early)
    middle = nz // 2
    from_below, from_above, early_parts = lax.optimization_barrier(
        (held[middle + 1], held[middle - 1], early_parts)
    )
    cut = max(nheads // 2, 1)
    held[middle] = jnp.concatenate(
        [
            lax.ppermute(from_below[:cut], "z", up),
            lax.ppermute(from_above[cut:], "z", down),
        ],
        0,
    )
    first = over_heads(early_parts, early)
    second = over_heads(parts_of(late), late)
    order = early + late
    done = jnp.concatenate([first, second], 2)
    done = unroll(jnp.stack([done[:, :, order.index(k)] for k in range(nz)], 0), 0, z)
    done = done.reshape(nz, ny, 2, shards // nheads, slots // 2, -1)
    done = done.transpose(3, 1, 0, 2, 4, 5)
    return done.reshape(shards // nheads * convs * slots, -1)


def solution(mesh):
    blk, head = mesh.shape["blk"], mesh.shape["head"]
    fine = Mesh(mesh.devices.reshape(2, blk // 4, 2, head), ("y", "z", "core", "head"))
    blk = ("y", "z", "core")
    return jax.shard_map(
        body,
        mesh=fine,
        in_specs=(
            P(blk, "head", None),
            P(blk, "head", None),
            P(blk, "head", None),
            P(blk, None, "head", None, None),
            P(blk, None, "head", None, None),
            P(blk, None),
            P(),
            P(),
            P("head", blk),
        ),
        out_specs=P("head", blk),
        check_vma=False,
    )
```

time: 224 us -> 254 us (1.13)
  waiting for transfers between devices: 49.8 us -> 118 us
  blocking collectives: 0 us -> 25.8 us
  other arithmetic: 38.5 us -> 14.7 us
  starting transfers between devices: 81.1 us -> 60.1 us
  Pallas kernels: 32.5 us -> 22.2 us
  local copies, waits for them, and re-layouts: 9.52 us -> 6.08 us
  matrix products: 10.1 us -> 6.74 us
    ppermute x20, waiting for transfers between devices: 6.03 us -> 86.5 us  [the longest x15 44.5 us: leg(): return lax.ppermute(block, ('y', 'z'), route)]
    all_to_all x0 -> x1, blocking collectives: none -> 25.8 us  [over_heads(): got = lax.all_to_all(parts, ('y', 'core', 'head'), 0, 0, tiled=True)]
    concatenate x16 -> x3, other arithmetic: 17.6 us -> 3.25 us  [the longest x1 2.74 us: body(): kv = jnp.concatenate([cache_keys[0, :, 0], stored_value_rows[0, :, 0]], 1)]
    all_to_all x3 -> x2, starting transfers between devices: 25.1 us -> 10.7 us  [the longest x1 7 us: body(): kv = lax.all_to_all(kv, ('y', 'z'), 0, 0, tiled=True)]
    pallas_call x5 -> x2, Pallas kernels: 32.3 us -> 18.3 us  [attend(): pl.pallas_call(functools.partial(attend_kernel, as_message), in_specs=[pl...]
    another operation x8 -> x4, other arithmetic: 10.6 us -> 0.97 us  [the longest x4 9.65 us: lens_of(): return jnp.stack([own_lens[chip_at(-dy, -dz)] for dy, dz in group])]
    all_to_all x3 -> x2, waiting for transfers between devices: 28.8 us -> 20.2 us  [the longest x1 20.2 us: over_heads(): got = lax.all_to_all(parts, ('y', 'core', 'head'), 0, 0, tiled=True)]
    ppermute x3, starting transfers between devices: 7.33 us -> 1.79 us  [body(): held[-step % nz] = lax.ppermute(held[(1 - step) % nz], 'z', up)]
  transfers between devices with their start and end apart: 31 -> 30, of which waited for: 8 -> 12; matrix products, arithmetic and copies ran while one was open for 21% -> 8% of each run, Pallas kernels for 15% -> 9%
where the time goes in v2:
time: 254 us
  waiting for transfers between devices  118 us (46%)
  starting transfers between devices  60.1 us (24%)
  blocking collectives  25.8 us (10%)
  Pallas kernels  22.2 us (9%)
  other arithmetic  14.7 us (6%)
  matrix products  6.74 us (3%)
  local copies, waits for them, and re-layouts  6.08 us (2%)
    ppermute x15, waiting for transfers between devices, leg(): return lax.ppermute(block, ('y', 'z'), route)  44.5 us
    ppermute x1, waiting for transfers between devices, body(): weight_y = lax.ppermute(weight, 'y', [(0, 1), (1, 0)])  40 us
    ppermute x15, starting transfers between devices, leg(): return lax.ppermute(block, ('y', 'z'), route)  32.3 us
    all_to_all x1, blocking collectives, over_heads(): got = lax.all_to_all(parts, ('y', 'core', 'head'), 0, 0, tiled=True)  25.8 us
    all_to_all x1, waiting for transfers between devices, over_heads(): got = lax.all_to_all(parts, ('y', 'core', 'head'), 0, 0, tiled=True)  20.2 us
    pallas_call x2, Pallas kernels, attend(): pl.pallas_call(functools.partial(attend_kernel, as_message), in_specs=[pl...  18.3 us
    ppermute x3, waiting for transfers between devices, body(): held[step] = lax.ppermute(held[step - 1], 'z', down)  7.68 us
    all_to_all x1, starting transfers between devices, body(): kv = lax.all_to_all(kv, ('y', 'z'), 0, 0, tiled=True)  7 us
  transfers between devices with their start and end apart: 30, of which 12 were waited for; matrix products, arithmetic and copies ran while one was open for 8% of the time, Pallas kernels for 9%

profile of v2, /device:TPU:1, one launch (start us, length us, event | category | flops | bytes accessed | tf_op | source)
XLA Modules:
  0.0 254.1 jit_solution(1453981027016793552)
XLA Ops:
  0.0 0.7 convert_bitcast_fusion.1
  0.8 1.0 pad_maximum_fusion.7
  2.0 6.5 %collective-permute-start = (bf16[80,128]{1,0:T(8,128)(2,1)S(1)}, bf16[80,128]{1,0:T(8,128)(2,1)S(1)}, u32[]{:S(2)}, u32[]{:S(2)}) collective-permute-start(bf16[80,128]{1,0:T(8,128)(2,1)S(1)} %get-tuple-element.41), channel_id=1, source_target_pairs={{16,0},{32,16},{48,32},{64,48},{80,64},{96,80},{112,96},{0,112},{1... | collective-permute-start | bytes 61448 | tf_op jit(solution)/shard_map/ppermute | solution.py:186
  8.5 1.2 collective-permute-start.1
  10.1 4.5 %collective-permute-start.3 = (bf16[80,128]{1,0:T(8,128)(2,1)S(1)}, bf16[80,128]{1,0:T(8,128)(2,1)S(1)}, u32[]{:S(2)}, u32[]{:S(2)}) collective-permute-start(bf16[80,128]{1,0:T(8,128)(2,1)S(1)} %get-tuple-element.38), channel_id=1, source_target_pairs={{64,0},{80,16},{96,32},{112,48},{0,64},{16,80},{32,96},{48,112},{1... | collective-permute-start | bytes 61448 | tf_op jit(solution)/shard_map/ppermute | solution.py:186
  14.6 2.7 %pad_maximum_fusion.1 = bf16[16,512,128]{2,1,0:T(8,128)(2,1)} fusion(bf16[16,256,128]{2,1,0:T(8,128)(2,1)S(1)} %bitcast.217, bf16[16,256,128]{2,1,0:T(8,128)(2,1)} %bitcast.218), kind=kLoop, calls=%fused_computation.1 | loop fusion | flops 4194304 | bytes 4194304 | tf_op jit(solution)/shard_map/concatenate | solution.py:163
  17.3 7.0 %all-to-all-start = ((bf16[16,512,128]{2,1,0:T(8,128)(2,1)}), bf16[16,512,128]{2,1,0:T(8,128)(2,1)S(1)}, u32[]{:S(2)}, u32[]{:S(2)}) async-start(bf16[16,512,128]{2,1,0:T(8,128)(2,1)} %pad_maximum_fusion.1), calls=%async_computation | async-start | bytes 4194304 | tf_op jit(solution)/shard_map/all_to_all | solution.py:164
  24.3 2.3 collective-permute-start.5
  26.7 1.3 collective-permute-start.6
  28.0 1.3 collective-permute-start.7
  29.3 1.6 collective-permute-start.8
  30.8 1.3 collective-permute-start.9
  32.1 40.2 %collective-permute-done.5 = bf16[80,128]{1,0:T(8,128)(2,1)S(1)} collective-permute-done((bf16[80,128]{1,0:T(8,128)(2,1)S(1)}, bf16[80,128]{1,0:T(8,128)(2,1)S(1)}, u32[]{:S(2)}, u32[]{:S(2)}) %collective-permute-start.5) | collective-permute-done | bytes 20512 | tf_op jit(solution)/shard_map/ppermute | solution.py:186
  72.3 4.5 %collective-permute-start.10 = (bf16[80,128]{1,0:T(8,128)(2,1)S(1)}, bf16[80,128]{1,0:T(8,128)(2,1)S(1)}, u32[]{:S(2)}, u32[]{:S(2)}) collective-permute-start(bf16[80,128]{1,0:T(8,128)(2,1)S(1)} %get-tuple-element.31), channel_id=1, source_target_pairs={{176,0},{192,16},{208,32},{224,48},{240,64},{128,80},{144,96},{160... | collective-permute-start | bytes 61448 | tf_op jit(solution)/shard_map/ppermute | solution.py:186
  76.9 0.9 collective-permute-start.11
  77.7 2.2 collective-permute-start.12
  80.0 3.2 %collective-permute-start.13 = (bf16[80,128]{1,0:T(8,128)(2,1)S(1)}, bf16[80,128]{1,0:T(8,128)(2,1)S(1)}, u32[]{:S(2)}, u32[]{:S(2)}) collective-permute-start(bf16[80,128]{1,0:T(8,128)(2,1)S(1)} %get-tuple-element.28), channel_id=1, source_target_pairs={{224,0},{240,16},{128,32},{144,48},{160,64},{176,80},{192,96},{208... | collective-permute-start | bytes 61448 | tf_op jit(solution)/shard_map/ppermute | solution.py:186
  83.2 1.2 collective-permute-start.14
  85.0 0.7 collective-permute-done.13
  85.7 2.9 %collective-permute-done.14 = bf16[80,128]{1,0:T(8,128)(2,1)S(1)} collective-permute-done((bf16[80,128]{1,0:T(8,128)(2,1)S(1)}, bf16[80,128]{1,0:T(8,128)(2,1)S(1)}, u32[]{:S(2)}, u32[]{:S(2)}) %collective-permute-start.14) | collective-permute-done | bytes 20512 | tf_op jit(solution)/shard_map/ppermute | solution.py:186
  88.7 4.8 %collective-permute-start.15 = (bf16[2,8,80,128]{3,2,1,0:T(8,128)(2,1)S(1)}, bf16[2,8,80,128]{3,2,1,0:T(8,128)(2,1)S(1)}, u32[]{:S(2)}, u32[]{:S(2)}) collective-permute-start(bf16[2,8,80,128]{3,2,1,0:T(8,128)(2,1)S(1)} %bitcast.224), channel_id=1, source_target_pairs={{0,8},{8,0},{1,9},{9,1},{2,10},{10,2},{3,11},{11,3},{4,12},{12,4},... | collective-permute-start | bytes 983048 | tf_op jit(solution)/shard_map/ppermute | solution.py:195
  93.5 1.3 collective-permute-done.15
  94.8 1.2 collective-permute-start.24
  96.5 1.3 fusion.9
  97.9 0.7 fusion.10
  98.9 0.7 collective-permute-start.23
  101.9 40.0 %collective-permute-done.24 = bf16[2048,512]{1,0:T(8,128)(2,1)} collective-permute-done((bf16[2048,512]{1,0:T(8,128)(2,1)}, bf16[2048,512]{1,0:T(8,128)(2,1)}, u32[]{:S(2)}, u32[]{:S(2)}) %collective-permute-start.24) | collective-permute-done | bytes 2097184 | tf_op jit(solution)/shard_map/ppermute | solution.py:198
  141.9 1.2 collective-permute-start.25
  144.8 1.4 copy.93
  147.1 1.3 fusion.5
  148.5 9.3 %shard_map.92 = bf16[1024,256]{1,0:T(8,128)(2,1)S(1)} custom-call(s32[16]{0:T(128)S(1)} %convert_reduce_fusion.1.lens_ref, bf16[1024,128]{1,0:T(8,128)(2,1)S(1)} %get-tuple-element.23.q_ref, bf16[16,512,128]{2,1,0:T(8,128)(2,1)S(1)} %all-to-all-done.kv_ref, bf16[128,128]{1,0:T(8,128)(2,1)S(1)} %pad_maximum_fusion.8.new_k_ref, ...), custom_call_target="tpu_custom_call" | custom-call | flops 4294967296 | bytes 4194304 | tf_op jit(solution)/shard_map/pallas_call | solution.py:89
  158.4 9.1 %shard_map.91 = (f32[1024,128]{1,0:T(8,128)S(1)}, f32[1024,128]{1,0:T(8,128)S(1)}) custom-call(s32[16]{0:T(128)S(1)} %convert_reduce_fusion.1.lens_ref, bf16[1024,128]{1,0:T(8,128)(2,1)S(1)} %get-tuple-element.24.q_ref, bf16[16,512,128]{2,1,0:T(8,128)(2,1)S(1)} %all-to-all-done.kv_ref, bf16[128,128]{1,0:T(8,128)(2,1)S(1)} %pad_maximum_fusion.8.new_k_ref, ...), custom_call_target="tpu_custom_call" | custom-call | flops 4294967296 | bytes 4194304 | tf_op jit(solution)/shard_map/pallas_call | solution.py:89
  167.6 3.9 %shard_map.93 = bf16[64,2048]{1,0:T(8,128)(2,1)S(1)} custom-call(f32[1024,128]{1,0:T(8,128)S(1)} %get-tuple-element.11.sums_ref, f32[1024,128]{1,0:T(8,128)S(1)} %get-tuple-element.12.stats_ref, bf16[1024,256]{1,0:T(8,128)(2,1)S(1)} %collective-permute-done.16.message_ref, f32[64,128]{1,0:T(8,128)S(1)} %broadcast_in_dim.43.live_ref), custom_call_target="tpu_custom_call" | custom-call | flops 524288 | bytes 1835008 | tf_op jit(solution)/shard_map/pallas_call | solution.py:126
  171.6 1.5 collective-permute-start.17
  173.1 3.2 %select_bitcast_fusion.3 = (bf16[1,2048,512]{2,1,0:T(8,128)(2,1)S(1)}, bf16[1,2048,512]{2,1,0:T(8,128)(2,1)S(1)}, bf16[1,2048,512]{2,1,0:T(8,128)(2,1)S(1)}, bf16[1,2048,512]{2,1,0:T(8,128)(2,1)S(1)}) fusion(pred[]{:T(512)S(6)} %eq.65, bf16[2048,512]{1,0:T(8,128)(2,1)S(1)} %copy-done, bf16[2048,512]{1,0:T(8,128)(2,1)} %collective-permute-done.23, ...), kind=kLoop, calls=%fused_computation.5 | loop fusion | flops 8388608 | bytes 16777218 | tf_op jit(solution)/shard_map/stack | solution.py:209
  176.3 2.7 %collective-permute-done.20 = bf16[8,8,2048]{2,1,0:T(8,128)(2,1)S(1)} collective-permute-done((bf16[8,8,2048]{2,1,0:T(8,128)(2,1)S(1)}, bf16[8,8,2048]{2,1,0:T(8,128)(2,1)S(1)}, u32[]{:S(2)}, u32[]{:S(2)}) %collective-permute-start.20) | collective-permute-done | bytes 262176 | tf_op jit(solution)/shard_map/ppermute | solution.py:272
  179.0 1.2 collective-permute-start.21
  180.4 5.0 %collective-permute-done.21 = bf16[8,8,2048]{2,1,0:T(8,128)(2,1)S(1)} collective-permute-done((bf16[8,8,2048]{2,1,0:T(8,128)(2,1)S(1)}, bf16[8,8,2048]{2,1,0:T(8,128)(2,1)S(1)}, u32[]{:S(2)}, u32[]{:S(2)}) %collective-permute-start.21) | collective-permute-done | bytes 262176 | tf_op jit(solution)/shard_map/ppermute | solution.py:272
  185.4 2.1 collective-permute-done.18
  187.8 2.7 %collective-permute-start.22 = (bf16[8,8,2048]{2,1,0:T(8,128)(2,1)S(1)}, bf16[8,8,2048]{2,1,0:T(8,128)(2,1)S(1)}, u32[]{:S(2)}, u32[]{:S(2)}) collective-permute-start(bf16[8,8,2048]{2,1,0:T(8,128)(2,1)S(1)} %collective-permute-done.21), channel_id=1, source_target_pairs={{0,112},{16,0},{32,16},{48,32},{64,48},{80,64},{96,80},{112,96},{1... | collective-permute-start | bytes 786440 | tf_op jit(solution)/shard_map/ppermute | solution.py:272
  190.5 4.3 %convolution_convert_fusion = bf16[4,512,320]{1,2,0:T(8,128)(2,1)} fusion(bf16[320,2048,1]{1,0,2:T(8,128)(2,1)S(1)} %bitcast.215, bf16[1,2048,512]{2,1,0:T(8,128)(2,1)S(1)} %get-tuple-element.20, bf16[1,2048,512]{2,1,0:T(8,128)(2,1)S(1)} %get-tuple-element.19, bf16[1,2048,512]{2,1,0:T(8,128)(2,1)S(1)} %get-tuple-element.18, ...), kind=kOutput, calls=%fused_computation.10 | convolution fusion | flops 2718564352 | bytes 11010048 | tf_op jit(solution)/shard_map/rk,wkn->wrn/dot_general | solution.py:276
  194.9 3.0 %collective-permute-start.27 = (bf16[4,8,2048]{2,1,0:T(8,128)(2,1)S(1)}, bf16[4,8,2048]{2,1,0:T(8,128)(2,1)S(1)}, u32[]{:S(2)}, u32[]{:S(2)}) collective-permute-start(bf16[4,8,2048]{2,1,0:T(8,128)(2,1)S(1)} %slice.66), channel_id=1, source_target_pairs={{0,112},{16,0},{32,16},{48,32},{64,48},{80,64},{96,80},{112,96},{1... | collective-permute-start | bytes 393224 | tf_op jit(solution)/shard_map/ppermute | solution.py:295
  197.9 2.0 collective-permute-done.26
  200.1 2.5 fusion.1
  202.6 25.8 %all_to_all.15 = bf16[32,24,512]{2,1,0:T(8,128)(2,1)S(1)} all-to-all(bf16[32,24,512]{2,1,0:T(8,128)(2,1)S(1)} %bitcast.220), channel_id=1, replica_groups=mesh['y'=2,'z'=8,'core'=2,'head'=8] {'y','core','head'}, dimensions={0} | all-to-all | bytes 1572864 | tf_op jit(solution)/shard_map/all_to_all | solution.py:280
  228.4 3.7 %all-to-all-start.1 = ((bf16[32,40,512]{2,1,0:T(8,128)(2,1)}), bf16[32,40,512]{2,1,0:T(8,128)(2,1)S(1)}, u32[]{:S(2)}, u32[]{:S(2)}) async-start(bf16[32,40,512]{2,1,0:T(8,128)(2,1)} %bitcast.76), calls=%async_computation.1 | async-start | bytes 2621440 | tf_op jit(solution)/shard_map/all_to_all | solution.py:280
  232.2 20.2 %all-to-all-done.1 = bf16[32,40,512]{2,1,0:T(8,128)(2,1)S(1)} async-done(((bf16[32,40,512]{2,1,0:T(8,128)(2,1)}), bf16[32,40,512]{2,1,0:T(8,128)(2,1)S(1)}, u32[]{:S(2)}, u32[]{:S(2)}) %all-to-all-start.1) | async-done | bytes 1310752 | tf_op jit(solution)/shard_map/all_to_all | solution.py:280
  253.3 0.8 reshape.139
  (122 shorter events, 9.5 us)
Async XLA Ops:
  0.0 14.6 %copy-start.1 = (bf16[1,16,1,256,128]{4,3,2,1,0:T(8,128)(2,1)S(1)}, bf16[1,16,1,256,128]{4,3,2,1,0:T(8,128)(2,1)}, u32[]{:S(2)}) copy-start(bf16[1,16,1,256,128]{4,3,2,1,0:T(8,128)(2,1)} %param.13) | copy-start | bytes 3145732
  2.0 22.3 %collective-permute-start = (bf16[80,128]{1,0:T(8,128)(2,1)S(1)}, bf16[80,128]{1,0:T(8,128)(2,1)S(1)}, u32[]{:S(2)}, u32[]{:S(2)}) collective-permute-start(bf16[80,128]{1,0:T(8,128)(2,1)S(1)} %get-tuple-element.41), channel_id=1, source_target_pairs={{16,0},{32,16},{48,32},{64,48},{80,64},{96,80},{112,96},{0,112},{1... | collective-permute-start | bytes 61448 | tf_op jit(solution)/shard_map/ppermute | solution.py:186
  8.5 18.2 %collective-permute-start.1 = (bf16[80,128]{1,0:T(8,128)(2,1)S(1)}, bf16[80,128]{1,0:T(8,128)(2,1)S(1)}, u32[]{:S(2)}, u32[]{:S(2)}) collective-permute-start(bf16[80,128]{1,0:T(8,128)(2,1)S(1)} %get-tuple-element.40), channel_id=1, source_target_pairs={{32,0},{48,16},{64,32},{80,48},{96,64},{112,80},{0,96},{16,112},{1... | collective-permute-start | bytes 61448 | tf_op jit(solution)/shard_map/ppermute | solution.py:186
  9.7 18.3 %collective-permute-start.2 = (bf16[80,128]{1,0:T(8,128)(2,1)S(1)}, bf16[80,128]{1,0:T(8,128)(2,1)S(1)}, u32[]{:S(2)}, u32[]{:S(2)}) collective-permute-start(bf16[80,128]{1,0:T(8,128)(2,1)S(1)} %get-tuple-element.39), channel_id=1, source_target_pairs={{48,0},{64,16},{80,32},{96,48},{112,64},{0,80},{16,96},{32,112},{1... | collective-permute-start | bytes 61448 | tf_op jit(solution)/shard_map/ppermute | solution.py:186
  10.1 19.2 %collective-permute-start.3 = (bf16[80,128]{1,0:T(8,128)(2,1)S(1)}, bf16[80,128]{1,0:T(8,128)(2,1)S(1)}, u32[]{:S(2)}, u32[]{:S(2)}) collective-permute-start(bf16[80,128]{1,0:T(8,128)(2,1)S(1)} %get-tuple-element.38), channel_id=1, source_target_pairs={{64,0},{80,16},{96,32},{112,48},{0,64},{16,80},{32,96},{48,112},{1... | collective-permute-start | bytes 61448 | tf_op jit(solution)/shard_map/ppermute | solution.py:186
  14.6 16.2 %collective-permute-start.4 = (bf16[80,128]{1,0:T(8,128)(2,1)S(1)}, bf16[80,128]{1,0:T(8,128)(2,1)S(1)}, u32[]{:S(2)}, u32[]{:S(2)}) collective-permute-start(bf16[80,128]{1,0:T(8,128)(2,1)S(1)} %get-tuple-element.37), channel_id=1, source_target_pairs={{80,0},{96,16},{112,32},{0,48},{16,64},{32,80},{48,96},{64,112},{2... | collective-permute-start | bytes 61448 | tf_op jit(solution)/shard_map/ppermute | solution.py:186
  17.3 78.6 %copy-start.2 = (s32[16]{0:T(128)S(1)}, s32[16]{0:T(128)}, u32[]{:S(2)}) copy-start(s32[16]{0:T(128)} %param.15) | copy-start | bytes 196
  17.3 131.1 %all-to-all-start = ((bf16[16,512,128]{2,1,0:T(8,128)(2,1)}), bf16[16,512,128]{2,1,0:T(8,128)(2,1)S(1)}, u32[]{:S(2)}, u32[]{:S(2)}) async-start(bf16[16,512,128]{2,1,0:T(8,128)(2,1)} %pad_maximum_fusion.1), calls=%async_computation | async-start | bytes 4194304 | tf_op jit(solution)/shard_map/all_to_all | solution.py:164
  24.3 47.9 %collective-permute-start.5 = (bf16[80,128]{1,0:T(8,128)(2,1)S(1)}, bf16[80,128]{1,0:T(8,128)(2,1)S(1)}, u32[]{:S(2)}, u32[]{:S(2)}) collective-permute-start(bf16[80,128]{1,0:T(8,128)(2,1)S(1)} %get-tuple-element.36), channel_id=1, source_target_pairs={{96,0},{112,16},{0,32},{16,48},{32,64},{48,80},{64,96},{80,112},{2... | collective-permute-start | bytes 61448 | tf_op jit(solution)/shard_map/ppermute | solution.py:186
  26.7 50.2 %collective-permute-start.6 = (bf16[80,128]{1,0:T(8,128)(2,1)S(1)}, bf16[80,128]{1,0:T(8,128)(2,1)S(1)}, u32[]{:S(2)}, u32[]{:S(2)}) collective-permute-start(bf16[80,128]{1,0:T(8,128)(2,1)S(1)} %get-tuple-element.35), channel_id=1, source_target_pairs={{112,0},{0,16},{16,32},{32,48},{48,64},{64,80},{80,96},{96,112},{2... | collective-permute-start | bytes 61448 | tf_op jit(solution)/shard_map/ppermute | solution.py:186
  28.0 49.8 %collective-permute-start.7 = (bf16[80,128]{1,0:T(8,128)(2,1)S(1)}, bf16[80,128]{1,0:T(8,128)(2,1)S(1)}, u32[]{:S(2)}, u32[]{:S(2)}) collective-permute-start(bf16[80,128]{1,0:T(8,128)(2,1)S(1)} %get-tuple-element.34), channel_id=1, source_target_pairs={{128,0},{144,16},{160,32},{176,48},{192,64},{208,80},{224,96},{240... | collective-permute-start | bytes 61448 | tf_op jit(solution)/shard_map/ppermute | solution.py:186
  29.3 50.7 %collective-permute-start.8 = (bf16[80,128]{1,0:T(8,128)(2,1)S(1)}, bf16[80,128]{1,0:T(8,128)(2,1)S(1)}, u32[]{:S(2)}, u32[]{:S(2)}) collective-permute-start(bf16[80,128]{1,0:T(8,128)(2,1)S(1)} %get-tuple-element.33), channel_id=1, source_target_pairs={{144,0},{160,16},{176,32},{192,48},{208,64},{224,80},{240,96},{128... | collective-permute-start | bytes 61448 | tf_op jit(solution)/shard_map/ppermute | solution.py:186
  30.8 52.3 %collective-permute-start.9 = (bf16[80,128]{1,0:T(8,128)(2,1)S(1)}, bf16[80,128]{1,0:T(8,128)(2,1)S(1)}, u32[]{:S(2)}, u32[]{:S(2)}) collective-permute-start(bf16[80,128]{1,0:T(8,128)(2,1)S(1)} %get-tuple-element.32), channel_id=1, source_target_pairs={{160,0},{176,16},{192,32},{208,48},{224,64},{240,80},{128,96},{144... | collective-permute-start | bytes 61448 | tf_op jit(solution)/shard_map/ppermute | solution.py:186
  72.3 12.1 %collective-permute-start.10 = (bf16[80,128]{1,0:T(8,128)(2,1)S(1)}, bf16[80,128]{1,0:T(8,128)(2,1)S(1)}, u32[]{:S(2)}, u32[]{:S(2)}) collective-permute-start(bf16[80,128]{1,0:T(8,128)(2,1)S(1)} %get-tuple-element.31), channel_id=1, source_target_pairs={{176,0},{192,16},{208,32},{224,48},{240,64},{128,80},{144,96},{160... | collective-permute-start | bytes 61448 | tf_op jit(solution)/shard_map/ppermute | solution.py:186
  76.9 7.6 %collective-permute-start.11 = (bf16[80,128]{1,0:T(8,128)(2,1)S(1)}, bf16[80,128]{1,0:T(8,128)(2,1)S(1)}, u32[]{:S(2)}, u32[]{:S(2)}) collective-permute-start(bf16[80,128]{1,0:T(8,128)(2,1)S(1)} %get-tuple-element.30), channel_id=1, source_target_pairs={{192,0},{208,16},{224,32},{240,48},{128,64},{144,80},{160,96},{176... | collective-permute-start | bytes 61448 | tf_op jit(solution)/shard_map/ppermute | solution.py:186
  77.7 7.3 %collective-permute-start.12 = (bf16[80,128]{1,0:T(8,128)(2,1)S(1)}, bf16[80,128]{1,0:T(8,128)(2,1)S(1)}, u32[]{:S(2)}, u32[]{:S(2)}) collective-permute-start(bf16[80,128]{1,0:T(8,128)(2,1)S(1)} %get-tuple-element.29), channel_id=1, source_target_pairs={{208,0},{224,16},{240,32},{128,48},{144,64},{160,80},{176,96},{192... | collective-permute-start | bytes 61448 | tf_op jit(solution)/shard_map/ppermute | solution.py:186
  80.0 5.7 %collective-permute-start.13 = (bf16[80,128]{1,0:T(8,128)(2,1)S(1)}, bf16[80,128]{1,0:T(8,128)(2,1)S(1)}, u32[]{:S(2)}, u32[]{:S(2)}) collective-permute-start(bf16[80,128]{1,0:T(8,128)(2,1)S(1)} %get-tuple-element.28), channel_id=1, source_target_pairs={{224,0},{240,16},{128,32},{144,48},{160,64},{176,80},{192,96},{208... | collective-permute-start | bytes 61448 | tf_op jit(solution)/shard_map/ppermute | solution.py:186
  83.2 5.5 %collective-permute-start.14 = (bf16[80,128]{1,0:T(8,128)(2,1)S(1)}, bf16[80,128]{1,0:T(8,128)(2,1)S(1)}, u32[]{:S(2)}, u32[]{:S(2)}) collective-permute-start(bf16[80,128]{1,0:T(8,128)(2,1)S(1)} %get-tuple-element.27), channel_id=1, source_target_pairs={{240,0},{128,16},{144,32},{160,48},{176,64},{192,80},{208,96},{224... | collective-permute-start | bytes 61448 | tf_op jit(solution)/shard_map/ppermute | solution.py:186
  88.7 6.1 %collective-permute-start.15 = (bf16[2,8,80,128]{3,2,1,0:T(8,128)(2,1)S(1)}, bf16[2,8,80,128]{3,2,1,0:T(8,128)(2,1)S(1)}, u32[]{:S(2)}, u32[]{:S(2)}) collective-permute-start(bf16[2,8,80,128]{3,2,1,0:T(8,128)(2,1)S(1)} %bitcast.224), channel_id=1, source_target_pairs={{0,8},{8,0},{1,9},{9,1},{2,10},{10,2},{3,11},{11,3},{4,12},{12,4},... | collective-permute-start | bytes 983048 | tf_op jit(solution)/shard_map/ppermute | solution.py:195
  94.8 47.2 %collective-permute-start.24 = (bf16[2048,512]{1,0:T(8,128)(2,1)}, bf16[2048,512]{1,0:T(8,128)(2,1)}, u32[]{:S(2)}, u32[]{:S(2)}) collective-permute-start(bf16[2048,512]{1,0:T(8,128)(2,1)} %param.17), channel_id=1, source_target_pairs={{0,128},{128,0},{1,129},{129,1},{2,130},{130,2},{3,131},{131,3},{4... | collective-permute-start | bytes 6291464 | tf_op jit(solution)/shard_map/ppermute | solution.py:198
  98.9 74.1 %collective-permute-start.23 = (bf16[2048,512]{1,0:T(8,128)(2,1)}, bf16[2048,512]{1,0:T(8,128)(2,1)}, u32[]{:S(2)}, u32[]{:S(2)}) collective-permute-start(bf16[2048,512]{1,0:T(8,128)(2,1)} %param.17), channel_id=1, source_target_pairs={{0,8},{8,0},{1,9},{9,1},{2,10},{10,2},{3,11},{11,3},{4,12},{12,4},... | collective-permute-start | bytes 6291464 | tf_op jit(solution)/shard_map/ppermute | solution.py:199
  141.9 31.1 %collective-permute-start.25 = (bf16[2048,512]{1,0:T(8,128)(2,1)}, bf16[2048,512]{1,0:T(8,128)(2,1)}, u32[]{:S(2)}, u32[]{:S(2)}) collective-permute-start(bf16[2048,512]{1,0:T(8,128)(2,1)} %collective-permute-done.24), channel_id=1, source_target_pairs={{0,8},{8,0},{1,9},{9,1},{2,10},{10,2},{3,11},{11,3},{4,12},{12,4},... | collective-permute-start | bytes 6291464 | tf_op jit(solution)/shard_map/ppermute | solution.py:200
  157.8 9.7 %collective-permute-start.16 = (bf16[1024,256]{1,0:T(8,128)(2,1)S(1)}, bf16[1024,256]{1,0:T(8,128)(2,1)S(1)}, u32[]{:S(2)}, u32[]{:S(2)}) collective-permute-start(bf16[1024,256]{1,0:T(8,128)(2,1)S(1)} %shard_map.92), channel_id=1, source_target_pairs={{0,8},{8,0},{1,9},{9,1},{2,10},{10,2},{3,11},{11,3},{4,12},{12,4},... | collective-permute-start | bytes 1572872 | tf_op jit(solution)/shard_map/ppermute | solution.py:261
  167.5 5.5 %copy-start = (bf16[2048,512]{1,0:T(8,128)(2,1)S(1)}, bf16[2048,512]{1,0:T(8,128)(2,1)}, u32[]{:S(2)}) copy-start(bf16[2048,512]{1,0:T(8,128)(2,1)} %param.17) | copy-start | bytes 6291460
  171.5 7.5 %collective-permute-start.20 = (bf16[8,8,2048]{2,1,0:T(8,128)(2,1)S(1)}, bf16[8,8,2048]{2,1,0:T(8,128)(2,1)S(1)}, u32[]{:S(2)}, u32[]{:S(2)}) collective-permute-start(bf16[8,8,2048]{2,1,0:T(8,128)(2,1)S(1)} %bitcast.202), channel_id=1, source_target_pairs={{0,112},{16,0},{32,16},{48,32},{64,48},{80,64},{96,80},{112,96},{1... | collective-permute-start | bytes 786440 | tf_op jit(solution)/shard_map/ppermute | solution.py:272
  171.6 8.6 %collective-permute-start.17 = (bf16[8,8,2048]{2,1,0:T(8,128)(2,1)S(1)}, bf16[8,8,2048]{2,1,0:T(8,128)(2,1)S(1)}, u32[]{:S(2)}, u32[]{:S(2)}) collective-permute-start(bf16[8,8,2048]{2,1,0:T(8,128)(2,1)S(1)} %bitcast.203), channel_id=1, source_target_pairs={{0,16},{16,32},{32,48},{48,64},{64,80},{80,96},{96,112},{112,0},{1... | collective-permute-start | bytes 786440 | tf_op jit(solution)/shard_map/ppermute | solution.py:271
  179.0 6.5 %collective-permute-start.21 = (bf16[8,8,2048]{2,1,0:T(8,128)(2,1)S(1)}, bf16[8,8,2048]{2,1,0:T(8,128)(2,1)S(1)}, u32[]{:S(2)}, u32[]{:S(2)}) collective-permute-start(bf16[8,8,2048]{2,1,0:T(8,128)(2,1)S(1)} %collective-permute-done.20), channel_id=1, source_target_pairs={{0,112},{16,0},{32,16},{48,32},{64,48},{80,64},{96,80},{112,96},{1... | collective-permute-start | bytes 786440 | tf_op jit(solution)/shard_map/ppermute | solution.py:272
  180.2 7.4 %collective-permute-start.18 = (bf16[8,8,2048]{2,1,0:T(8,128)(2,1)S(1)}, bf16[8,8,2048]{2,1,0:T(8,128)(2,1)S(1)}, u32[]{:S(2)}, u32[]{:S(2)}) collective-permute-start(bf16[8,8,2048]{2,1,0:T(8,128)(2,1)S(1)} %collective-permute-done.17), channel_id=1, source_target_pairs={{0,16},{16,32},{32,48},{48,64},{64,80},{80,96},{96,112},{112,0},{1... | collective-permute-start | bytes 786440 | tf_op jit(solution)/shard_map/ppermute | solution.py:271
  187.7 7.0 %collective-permute-start.19 = (bf16[8,8,2048]{2,1,0:T(8,128)(2,1)S(1)}, bf16[8,8,2048]{2,1,0:T(8,128)(2,1)S(1)}, u32[]{:S(2)}, u32[]{:S(2)}) collective-permute-start(bf16[8,8,2048]{2,1,0:T(8,128)(2,1)S(1)} %collective-permute-done.18), channel_id=1, source_target_pairs={{0,16},{16,32},{32,48},{48,64},{64,80},{80,96},{96,112},{112,0},{1... | collective-permute-start | bytes 786440 | tf_op jit(solution)/shard_map/ppermute | solution.py:271
  187.8 6.9 %collective-permute-start.22 = (bf16[8,8,2048]{2,1,0:T(8,128)(2,1)S(1)}, bf16[8,8,2048]{2,1,0:T(8,128)(2,1)S(1)}, u32[]{:S(2)}, u32[]{:S(2)}) collective-permute-start(bf16[8,8,2048]{2,1,0:T(8,128)(2,1)S(1)} %collective-permute-done.21), channel_id=1, source_target_pairs={{0,112},{16,0},{32,16},{48,32},{64,48},{80,64},{96,80},{112,96},{1... | collective-permute-start | bytes 786440 | tf_op jit(solution)/shard_map/ppermute | solution.py:272
  194.8 5.1 %collective-permute-start.26 = (bf16[4,8,2048]{2,1,0:T(8,128)(2,1)S(1)}, bf16[4,8,2048]{2,1,0:T(8,128)(2,1)S(1)}, u32[]{:S(2)}, u32[]{:S(2)}) collective-permute-start(bf16[4,8,2048]{2,1,0:T(8,128)(2,1)S(1)} %slice.65), channel_id=1, source_target_pairs={{0,16},{16,32},{32,48},{48,64},{64,80},{80,96},{96,112},{112,0},{1... | collective-permute-start | bytes 393224 | tf_op jit(solution)/shard_map/ppermute | solution.py:294
  194.9 5.0 %collective-permute-start.27 = (bf16[4,8,2048]{2,1,0:T(8,128)(2,1)S(1)}, bf16[4,8,2048]{2,1,0:T(8,128)(2,1)S(1)}, u32[]{:S(2)}, u32[]{:S(2)}) collective-permute-start(bf16[4,8,2048]{2,1,0:T(8,128)(2,1)S(1)} %slice.66), channel_id=1, source_target_pairs={{0,112},{16,0},{32,16},{48,32},{64,48},{80,64},{96,80},{112,96},{1... | collective-permute-start | bytes 393224 | tf_op jit(solution)/shard_map/ppermute | solution.py:295
  228.4 24.1 %all-to-all-start.1 = ((bf16[32,40,512]{2,1,0:T(8,128)(2,1)}), bf16[32,40,512]{2,1,0:T(8,128)(2,1)S(1)}, u32[]{:S(2)}, u32[]{:S(2)}) async-start(bf16[32,40,512]{2,1,0:T(8,128)(2,1)} %bitcast.76), calls=%async_computation.1 | async-start | bytes 2621440 | tf_op jit(solution)/shard_map/all_to_all | solution.py:280
